TPU v7x, 32 devices: a whole 2x2x4 slice. The times are simulated.
32 devices in a mesh: plane: 2 (over x), span: 4 (over z), height: 4 (over y, core).
Axes of the slice: x: 2, y: 2, z: 4, core: 2. Of those that a mesh axis runs over, the one named last changes fastest.
Arguments:
- noisy: bfloat16 [2, 3, 256, 512], P('plane', None, 'height', 'span'), may hold values from -6 to 6
- coarse_cond: bfloat16 [32, 2, 3, 32, 64], P(('plane', 'span', 'height')), may hold values from -6 to 6
- timestep: int32 [1], replicated, may hold values from 20 to 899
- owner: int32 [1], replicated, may hold values from 0 to 31
- w_embed: float32 [64, 256], replicated, may hold values from -0.75 to 0.75
- w_biases: float32 [256, 448], replicated, may hold values from -0.375 to 0.375
- w_enter: bfloat16 [3, 64, 18], replicated, may hold values from -1.5 to 1.5
- pool_fine: bfloat16 [4, 128, 64], replicated, may hold values from -0.5 to 0.5
- pool_mid: bfloat16 [4, 256, 128], replicated, may hold values from -0.375 to 0.375
- w_squeeze: bfloat16 [128, 256], replicated, may hold values from -0.375 to 0.375
- w_across: bfloat16 [3, 256, 128], replicated, may hold values from -0.5 to 0.5
- w_middle: bfloat16 [3, 256, 768], replicated, may hold values from -0.21875 to 0.21875
- rise_mid: bfloat16 [4, 128, 256], replicated, may hold values from -0.5 to 0.5
- decode_mid: bfloat16 [3, 128, 384], replicated, may hold values from -0.3125 to 0.3125
- rise_fine: bfloat16 [4, 64, 128], replicated, may hold values from -0.75 to 0.75
- decode_fine: bfloat16 [3, 64, 192], replicated, may hold values from -0.4375 to 0.4375
- w_leave: bfloat16 [3, 3, 192], replicated, may hold values from -0.4375 to 0.4375
Outputs:
- noise_pred: bfloat16 [2, 3, 256, 512], P('plane', None, 'height', 'span')
- next_sample: float32 [2, 3, 256, 512], P('plane', None, 'height', 'span')
Inputs may be any that keep to these rules, and one draw needn't show every extreme that they name: The timestep lies in the plan's range and is at least 20. The owner is a device index in the mesh order plane, span, height.
All inputs are finite; a program needn't handle non-finite values.
Results may differ from a plain program's by a relative error of at most 0.03.
Values may be sent and summed in bfloat16 or wider, within the bound.
No kernel may reach another device: no remote copies, remote signals or barrier semaphores. Data moves between devices by JAX's collectives and lax.ppermute only.
A program may use at most 64 MiB of HBM per device.

v0:
```python
import math

import jax
import jax.numpy as jnp
import numpy as np
from jax import lax
from jax.experimental import pallas as pl
from jax.experimental.pallas import tpu as pltpu
from jax.sharding import PartitionSpec as P

CF = 8
TSTEPS = 1000
STRIDE = 20
RIM = 9
EDGE = 2
BF = jnp.bfloat16
F32 = jnp.float32
AXES = ("plane", "span", "height")


def up(n, m):
    return -(-n // m) * m


def dot(a, b):
    return jnp.dot(a, b, preferred_element_type=F32)


def dot_nt(a, b):
    return lax.dot_general(a, b, (((1,), (1,)), ((), ())), preferred_element_type=F32)


def silu(x):
    half = 0.5 * x
    return half + half * jnp.tanh(half)


class Sizes:
    def __init__(self, rows, cols, planes, spans, heights, cond_rows, cond_cols):
        self.rows, self.cols = rows, cols
        self.planes, self.spans, self.heights = planes, spans, heights
        self.cond_rows, self.cond_cols = cond_rows, cond_cols
        self.devices = planes * spans * heights
        self.gi, self.gj = rows // 4 + 2 * EDGE, cols // 4 + 2 * EDGE
        self.step = up(self.gj, 16)
        self.cells = self.gi * self.step
        self.slots = min(planes, 3)
        self.strip = up(3 * RIM, 16)
        self.ext = 2 * self.strip + 3 * rows
        self.patch_rows, self.patch_cols = rows // CF + 4, cols // CF + 4
        self.patch = up(self.patch_rows, 16)
        self.piece = self.strip + self.patch * ((self.slots + 1) // 2)

    def planes_of(self, plane):
        if self.planes == 1:
            return [plane]
        if self.planes == 2:
            return [plane, 1 - plane]
        return [plane, plane - 1, plane + 1]


def pack_constants(z):
    bottom = np.zeros((z.strip, 3 * z.rows), np.float32)
    top = np.zeros((z.strip, 3 * z.rows), np.float32)
    for c in range(3):
        for r in range(RIM):
            bottom[c * RIM + r, c * z.rows + z.rows - RIM + r] = 1
            top[c * RIM + r, c * z.rows + r] = 1
    sides = np.zeros((2 * 16, z.cols), np.float32)
    for r in range(RIM):
        sides[r, z.cols - RIM + r] = 1
        sides[16 + r, r] = 1
    window = np.zeros((3, z.cond_cols, z.spans * 128), np.float32)
    for s in range(z.spans):
        for x in range(z.patch_cols):
            col = s * (z.cols // CF) + x - 2
            if 0 <= col < z.cond_cols:
                for c in range(3):
                    window[c, col, s * 128 + c * z.patch_cols + x] = 1
    return np.concatenate([bottom, top]).astype(BF), sides.astype(BF), window.astype(BF)


def unpack_constants(z):
    across = np.zeros((z.cols + 128, 6 * 64), np.float32)
    lift = np.zeros((2, 3, 128, 6 * 64), np.float32)
    for b in range(6):
        for j in range(z.gj):
            col = 4 * (j - EDGE) - 1 + b
            if col < 0:
                across[z.cols + 128 + col, b * 64 + j] = 1
            elif col < z.cols:
                across[col, b * 64 + j] = 1
            else:
                across[z.cols + col - z.cols, b * 64 + j] = 1
            for half in range(2):
                for c in range(3):
                    lift[half, c, half * 64 + c * z.patch_cols + col // CF + 2, b * 64 + j] = 1
    down = np.zeros((z.gi * 40, z.ext + 3 * z.patch), np.float32)
    for i in range(z.gi):
        for c in range(3):
            for a in range(6):
                row = 4 * (i - EDGE) - 1 + a
                if row < 0:
                    source = c * RIM + row + RIM
                elif row < z.rows:
                    source = z.strip + c * z.rows + row
                else:
                    source = z.strip + 3 * z.rows + c * RIM + row - z.rows
                down[i * 40 + c * 6 + a, source] = 1
                down[i * 40 + 18 + c * 6 + a, z.ext + c * z.patch + row // CF + 2] = 1
    sides = np.zeros((2 * 16, 128), np.float32)
    for r in range(RIM):
        sides[r, 128 - RIM + r] = 1
        sides[16 + r, r] = 1
    spread = np.zeros((2 * z.step, 2 * z.cols), np.float32)
    for pair in range(2):
        for j in range(z.cols // 4):
            for b in range(2):
                spread[pair * z.step + j + EDGE, b * z.cols + 4 * j + 2 * pair + b] = 1
    inner = z.rows // 4
    gather = np.zeros((2, 3 * z.rows, inner * 24), np.float32)
    for b in range(2):
        for i in range(inner):
            for a in range(4):
                for o in range(3):
                    gather[b, o * z.rows + 4 * i + a, i * 24 + a * 6 + b * 3 + o] = 1
    return tuple(
        m.astype(BF) for m in (across, lift.reshape(-1, 6 * 64), down, sides, spread, gather)
    )


def pack_kernel(z, noisy, slot, strips, sides, window, send, padded):
    plane, span, height = (lax.axis_index(a) for a in AXES)
    tile = noisy[0].reshape(3 * z.rows, z.cols)
    ends = dot(strips[...], tile).astype(BF)
    cols = dot_nt(sides[...], tile).astype(BF)
    wide = None
    for c in range(3):
        part = dot(slot[0, :, c].reshape(z.planes * z.cond_rows, z.cond_cols), window[c])
        wide = part if wide is None else wide + part
    padded[...] = jnp.zeros_like(padded)
    for p in range(z.planes):
        padded[p, 2 : 2 + z.cond_rows, :] = wide[p * z.cond_rows : (p + 1) * z.cond_rows]
    send[:, 0 : z.strip, :] = jnp.zeros((z.devices, z.strip, 128), BF)
    tall = z.rows // CF
    for p in range(z.planes):
        for s in range(z.spans):
            for h in range(z.heights):
                target = (p * z.spans + s) * z.heights + h
                for k0 in range(0, z.slots, 2):
                    both = None
                    for k in range(k0, min(k0 + 2, z.slots)):
                        q = z.planes_of(p)[k]
                        if 0 <= q < z.planes:
                            part = padded[
                                q, tall * h : tall * h + z.patch, s * 128 : (s + 1) * 128
                            ]
                            part = part if k == k0 else pltpu.roll(part, 64, 1)
                            both = part if both is None else both + part
                    if both is None:
                        both = jnp.zeros((z.patch, 128), F32)
                    base = z.strip + k0 // 2 * z.patch
                    send[target, base : base + z.patch, :] = both.astype(BF)
    for k in range(z.slots):
        q = z.planes_of(plane)[k]
        for dh in (-1, 0, 1):
            for ds in (-1, 0, 1):
                if dh == 0 and ds == 0:
                    continue
                ok = (
                    (q >= 0) & (q < z.planes)
                    & (span + ds >= 0) & (span + ds < z.spans)
                    & (height + dh >= 0) & (height + dh < z.heights)
                )

                @pl.when(ok)
                def _(q=q, dh=dh, ds=ds):
                    target = (q * z.spans + span + ds) * z.heights + height + dh
                    if dh != 0:
                        half = 0 if dh > 0 else z.strip
                        send[target, 0 : z.strip, :] = ends[half : half + z.strip]
                    else:
                        half = 0 if ds > 0 else 16
                        send[target, 0:16, :] = cols[half : half + 16, 0:128]
                        send[target, 16:32, 0:64] = cols[half : half + 16, 128:192]


def net_kernel(
    z, owner, coefs, noisy, others, recv, bias,
    across, lift, down, sides, spread, gather,
    w_in, w_pf, w_pm, w_sq, w_ac, w_mid, w_rm, w_dm, w_rf, w_df, w_lv,
    pred, sample,
    ext, grid, entry, h1, d1, d2, sq, mx, v2, v1, e1, last, mask, half, halfp,
):
    plane, span, height = (lax.axis_index(a) for a in AXES)
    step, gi = z.step, z.gi
    n1, n2, n3 = w_in.shape[1] // 16, w_pf.shape[1], w_pm.shape[1]
    inner = z.rows // 4

    shape = (gi, step, 128)
    row = lax.broadcasted_iota(jnp.int32, shape, 0) + (height * inner - EDGE)
    col = lax.broadcasted_iota(jnp.int32, shape, 1) + (span * (z.cols // 4) - EDGE)
    lane = lax.broadcasted_iota(jnp.int32, shape, 2)
    row_in = (row >= 0) & (row < z.heights * inner)
    wide = z.spans * (z.cols // 4)
    here = row_in & (col >= 0) & (col < wide)
    colp = col + jnp.where(lane >= n1, 1, 0)
    herep = row_in & (colp >= 0) & (colp < wide)
    mask[...] = jnp.where(here, 1.0, 0.0).reshape(z.cells, 128)
    half[...] = jnp.where(here, 0.5, 0.0).reshape(z.cells, 128)
    halfp[...] = jnp.where(herep, 0.5, 0.0).reshape(z.cells, 128)

    def masked(x, rows, ref=mask):
        m = ref[rows, :]
        return x * jnp.concatenate([m] * (x.shape[1] // 128), axis=1)

    lanes = lax.broadcasted_iota(jnp.int32, (z.strip, 128), 1)
    b1 = bias[:, 0:n1]
    b1 = jnp.concatenate([b1] * 4, axis=1)
    b2 = bias[:, n1 : n1 + n2]
    b3 = bias[:, n1 + n2 : n1 + n2 + n3]

    for k in range(z.slots):
        q = z.planes_of(plane)[k]

        def piece(dh, ds, q=q):
            ok = (
                (q >= 0) & (q < z.planes)
                & (span + ds >= 0) & (span + ds < z.spans)
                & (height + dh >= 0) & (height + dh < z.heights)
            )
            source = (q * z.spans + span + ds) * z.heights + height + dh
            source = jnp.clip(source, 0, z.devices - 1)
            value = recv[source, 0 : z.strip, :].astype(F32)
            return jnp.where(ok, value, 0.0)

        tile = (noisy[0] if k == 0 else others[k - 1]).reshape(3 * z.rows, z.cols)
        ext[z.strip : z.strip + 3 * z.rows, 0 : z.cols] = tile
        for dh, base in ((-1, 0), (1, z.strip + 3 * z.rows)):
            ext[base : base + z.strip, 0 : z.cols] = piece(dh, 0).astype(BF)
            left, right = piece(dh, -1), piece(dh, 1)
            rim = jnp.where(lanes >= 128 - RIM, left, jnp.where(lanes < RIM, right, 0.0))
            ext[base : base + z.strip, z.cols : z.cols + 128] = rim.astype(BF)
        left, right = piece(0, -1), piece(0, 1)
        halves = [
            jnp.concatenate([v[0:16], v[16:32]], axis=1) for v in (left, right)
        ]
        rims = jnp.concatenate(halves, axis=0)
        rims = jnp.transpose(rims)[0 : 3 * z.rows].astype(BF)
        ext[z.strip : z.strip + 3 * z.rows, z.cols : z.cols + 128] = dot(
            rims, sides[...]
        ).astype(BF)
        base = z.strip + k // 2 * z.patch
        patch = recv[owner[0], base : base + z.patch, :]
        wide_rows = [dot(ext[...], across[...]).astype(BF)]
        for c in range(3):
            at = (k % 2 * 3 + c) * 128
            wide_rows.append(dot(patch, lift[at : at + 128, :]).astype(BF))
        grid[...] = dot(down[...], jnp.concatenate(wide_rows, axis=0))
        for i in range(gi):
            block = grid[i * 40 : (i + 1) * 40, :]
            stack = jnp.concatenate(
                [block[:, 0:128], block[:, 128:256], block[:, 256:384], jnp.zeros((8, 128), F32)],
                axis=0,
            )
            turned = jnp.transpose(stack)
            at = i * step
            entry[at : at + step, 0:128] = turned[0:step].astype(BF)
            entry[at : at + step, 128:256] = turned[64 : 64 + step].astype(BF)
        per = 5 if gi % 5 == 0 else 1
        for i in range(0, gi, per):
            rows = slice(i * step, (i + per) * step)
            x = entry[rows, :]
            mids = []
            for g in range(4):
                h = dot(x, w_in[:, g * 4 * n1 : (g + 1) * 4 * n1]) + b1
                h = silu(h).astype(BF)
                if k == 0:
                    h1[g, rows, :] = h
                m = silu(dot(h, w_pf[...]) + b2).astype(BF)
                if k == 0:
                    d1[rows, g * n2 : (g + 1) * n2] = m
                mids.append(m)
            low = silu(dot(jnp.concatenate(mids, axis=1), w_pm[...]) + b3).astype(BF)
            if k == 0:
                d2[rows, :] = low
            width = w_sq.shape[1]
            sq[rows, k * width : (k + 1) * width] = dot(low, w_sq[...]).astype(BF)

    def chunks(first, last_, per):
        out = []
        while first < last_:
            out.append((first, min(per, last_ - first)))
            first += per
        return out

    def span_of(i, n, shift=0):
        return slice((i + shift) * step, (i + shift + n) * step)

    for i, n in chunks(0, gi, 5):
        rows = span_of(i, n)
        m = d2[rows, :].astype(F32) + dot(sq[rows, :], w_ac[...])
        m = masked(m, rows)
        mx[rows, n3 : 2 * n3] = m.astype(BF)
        mx[rows, 0:n3] = pltpu.roll(m, 1, 0).astype(BF)
        mx[rows, 2 * n3 : 3 * n3] = pltpu.roll(m, n * step - 1, 0).astype(BF)

    for i, n in chunks(1, gi - 1, 6):
        rows = span_of(i, n)
        c = None
        for a in range(3):
            part = dot(mx[span_of(i, n, a - 1), :], w_mid[a])
            c = part if c is None else c + part
        c = silu(c).astype(BF)
        v = dot(c, w_rm[...]) + d1[rows, :].astype(F32)
        v = masked(v, rows)
        for p in range(2):
            vp = v[:, 2 * p * n2 : 2 * (p + 1) * n2]
            v2[p, rows, n2 : 3 * n2] = vp.astype(BF)
            v2[p, rows, 0:n2] = pltpu.roll(vp[:, n2:], 1, 0).astype(BF)
            v2[p, rows, 3 * n2 : 4 * n2] = pltpu.roll(vp[:, :n2], n * step - 1, 0).astype(BF)

    for p in range(2):
        for i, n in chunks(2 - p, gi - 1 - p, 6):
            rows = span_of(i, n)
            e = None
            for a in range(3):
                at = p + a - 1
                part = dot(v2[at % 2, span_of(i, n, at // 2), :], w_dm[a])
                e = part if e is None else e + part
            e = silu(e).astype(BF)
            for q in range(2):
                v = dot(e[:, q * n2 : (q + 1) * n2], w_rf[...])
                v = masked(v + h1[2 * p + q, rows, :].astype(F32), rows)
                for a in range(2):
                    va = v[:, 2 * a * n1 : 2 * (a + 1) * n1]
                    v1[2 * p + a, rows, 2 * q * n1 : 2 * (q + 1) * n1] = va.astype(BF)
                    if q == 0:
                        v1[2 * p + a, rows, 4 * n1 : 6 * n1] = pltpu.roll(
                            va, n * step - 1, 0
                        ).astype(BF)

    for turn in range(2):
        for i, n in chunks(2 - turn, gi - 2, 6):
            rows = span_of(i, n)
            for pair in range(2):
                x = None
                for a in range(4):
                    at = 2 * turn + a
                    part = dot(
                        v1[at % 4, span_of(i, n, at // 4), 2 * pair * n1 : (2 * pair + 4) * n1],
                        w_df[a],
                    )
                    x = part if x is None else x + part
                for a in range(2):
                    at = 2 * turn + 1 + a
                    there = span_of(i, n, at // 4)
                    t = masked(
                        x[:, 2 * a * n1 : 2 * (a + 1) * n1], there, halfp if pair else half
                    )
                    t = t + t * jnp.tanh(t)
                    if pair == 0:
                        e1[at % 4, there, 2 * n1 : 4 * n1] = t.astype(BF)
                    else:
                        e1[at % 4, there, 4 * n1 : 6 * n1] = t.astype(BF)
                        e1[at % 4, there, 0 : 2 * n1] = pltpu.roll(t, 1, 0).astype(BF)

    for i, n in chunks(2, gi - 2, 8):
        outs = []
        for pair in range(2):
            x = None
            for a in range(6):
                at = a - 1
                part = dot(
                    e1[at % 4, span_of(i, n, at // 4), 2 * pair * n1 : (2 * pair + 4) * n1],
                    w_lv[a],
                )
                x = part if x is None else x + part
            outs.append(x)
        for r in range(n):
            block = jnp.concatenate([o[r * step : (r + 1) * step] for o in outs], axis=0)
            turned = jnp.transpose(block)[0:24]
            at = (i - 2 + r) * 24
            last[at : at + 24, :] = turned
    spread_out = dot(last[...].astype(BF), spread[...]).astype(BF)
    guess = dot(gather[0], spread_out[:, 0 : z.cols])
    guess = guess + dot(gather[1], spread_out[:, z.cols :])
    pred[0] = guess.astype(BF).reshape(3, z.rows, z.cols)
    given = noisy[0].reshape(3 * z.rows, z.cols).astype(F32)
    clean = (given - coefs[0] * guess) * coefs[1]
    result = coefs[2] * clean + coefs[3] * guess
    sample[0] = result.reshape(3, z.rows, z.cols)


def plan(stepnum):
    phase = (stepnum.astype(F32) / TSTEPS + 0.008) / 1.008 * (math.pi / 2.0)
    return jnp.cos(phase) ** 2


def time_bias(timestep, w_embed, w_biases):
    half = w_embed.shape[0] // 2
    freqs = jnp.exp(-math.log(10000.0) * jnp.arange(half, dtype=F32) / half)
    angles = timestep[0].astype(F32) * freqs
    waves = jnp.concatenate([jnp.sin(angles), jnp.cos(angles)])
    hidden = jax.nn.silu(jnp.dot(waves, w_embed, precision=lax.Precision.HIGHEST))
    return jnp.dot(hidden, w_biases, precision=lax.Precision.HIGHEST)


def lay_weights(
    z, plane, w_enter, pool_fine, pool_mid, w_squeeze, w_across, w_middle,
    rise_mid, decode_mid, rise_fine, decode_fine, w_leave,
):
    n1, n2, n3 = w_enter.shape[1], pool_fine.shape[1], pool_mid.shape[1]
    w = w_enter.reshape(3, n1, 3, 6).transpose(0, 2, 3, 1)
    parts = []
    for p in range(2):
        for q in range(2):
            for a in range(2):
                for b in range(2):
                    y, x = 2 * p + a, 2 * q + b
                    parts.append(jnp.pad(w, ((y, 3 - y), (x, 3 - x), (0, 0), (0, 0))))
    w = jnp.stack(parts, axis=3)
    w = w.reshape(6, 3, 2, 6, 16 * n1).transpose(2, 1, 3, 0, 4).reshape(2, 3, 36, 16 * n1)
    w = jnp.pad(w, ((0, 0), (0, 0), (0, 4), (0, 0))).reshape(2, 120, 16 * n1)
    w_in = jnp.pad(w, ((0, 0), (0, 8), (0, 0))).reshape(256, 16 * n1)
    w_pf = pool_fine.transpose(0, 2, 1).reshape(4 * n1, n2)
    w_pm = pool_mid.transpose(0, 2, 1).reshape(4 * n2, n3)
    taps = [w_across[1]]
    if z.planes == 2:
        taps.append(jnp.where(plane == 0, w_across[2], w_across[0]))
    elif z.planes > 2:
        taps.append(jnp.where(plane > 0, w_across[0], jnp.zeros_like(w_across[0])))
        taps.append(jnp.where(plane < z.planes - 1, w_across[2], jnp.zeros_like(w_across[2])))
    w_ac = jnp.concatenate([t.T for t in taps], axis=0)
    w_mid = w_middle.transpose(0, 2, 1)
    w_rm = rise_mid.transpose(2, 0, 1).reshape(n3, 4 * n2)
    w = decode_mid.transpose(0, 2, 1)
    w_dm = jnp.concatenate(
        [jnp.pad(w, ((0, 0), (q * n2, (1 - q) * n2), (0, 0))) for q in range(2)], axis=2
    )
    w_rf = rise_fine.transpose(2, 0, 1).reshape(n2, 4 * n1)
    w = decode_fine.transpose(0, 2, 1)
    w_df = jnp.concatenate(
        [
            jnp.pad(w, ((a, 1 - a), (b * n1, (1 - b) * n1), (0, 0)))
            for a in range(2)
            for b in range(2)
        ],
        axis=2,
    )
    w = w_leave.transpose(0, 2, 1)
    w_lv = jnp.concatenate(
        [
            jnp.pad(w, ((a, 3 - a), (b * n1, (1 - b) * n1), (0, 0)))
            for a in range(4)
            for b in range(2)
        ],
        axis=2,
    )
    w_lv = jnp.pad(w_lv, ((0, 0), (0, 0), (0, 128 - w_lv.shape[2])))
    return w_in, w_pf, w_pm, w_sq_t(w_squeeze), w_ac, w_mid, w_rm, w_dm, w_rf, w_df, w_lv


def w_sq_t(w_squeeze):
    return w_squeeze.T


def solution(mesh):
    planes, spans, heights = (mesh.shape[a] for a in AXES)

    def shards(
        noisy, coarse_cond, timestep, owner, w_embed, w_biases, w_enter, pool_fine, pool_mid,
        w_squeeze, w_across, w_middle, rise_mid, decode_mid, rise_fine, decode_fine, w_leave,
    ):
        rows, cols = noisy.shape[2:]
        z = Sizes(rows, cols, planes, spans, heights, *coarse_cond.shape[3:])
        n1, n2, n3 = w_enter.shape[1], pool_fine.shape[1], pool_mid.shape[1]
        vmem = pl.BlockSpec(memory_space=pltpu.VMEM)
        smem = pl.BlockSpec(memory_space=pltpu.SMEM)
        strips, sides, window = (jnp.asarray(m) for m in pack_constants(z))
        send = pl.pallas_call(
            lambda *refs: pack_kernel(z, *refs),
            out_shape=jax.ShapeDtypeStruct((z.devices, z.piece, 128), BF),
            in_specs=[vmem] * 5,
            out_specs=vmem,
            scratch_shapes=[
                pltpu.VMEM((planes, up(z.cond_rows + 4 + 8, 8), spans * 128), F32)
            ],
            compiler_params=pltpu.CompilerParams(vmem_limit_bytes=32 * 2**20),
            name="pack",
        )(noisy, coarse_cond, strips, sides, window)
        recv = lax.all_to_all(send, AXES, 0, 0, tiled=True)
        tile = noisy[0]
        if planes == 1:
            others = tile[None]
        elif planes == 2:
            others = lax.ppermute(tile, "plane", [(0, 1), (1, 0)])[None]
        else:
            ahead = [(i, i + 1) for i in range(planes - 1)]
            behind = [(i + 1, i) for i in range(planes - 1)]
            others = jnp.stack(
                [lax.ppermute(tile, "plane", ahead), lax.ppermute(tile, "plane", behind)]
            )
        plane = lax.axis_index("plane")
        bias = time_bias(timestep, w_embed, w_biases)[None]
        now, prior = plan(timestep[0]), plan(timestep[0] - STRIDE)
        coefs = jnp.stack(
            [jnp.sqrt(1.0 - now), 1.0 / jnp.sqrt(now), jnp.sqrt(prior), jnp.sqrt(1.0 - prior)]
        )
        weights = lay_weights(
            z, plane, w_enter, pool_fine, pool_mid, w_squeeze, w_across, w_middle,
            rise_mid, decode_mid, rise_fine, decode_fine, w_leave,
        )
        constants = [jnp.asarray(m) for m in unpack_constants(z)]
        operands = [owner, coefs, noisy, others, recv, bias, *constants, *weights]
        cells = z.cells
        return pl.pallas_call(
            lambda *refs: net_kernel(z, *refs),
            out_shape=(
                jax.ShapeDtypeStruct(noisy.shape, BF),
                jax.ShapeDtypeStruct(noisy.shape, F32),
            ),
            in_specs=[smem, smem] + [vmem] * (len(operands) - 2),
            out_specs=(vmem, vmem),
            scratch_shapes=[
                pltpu.VMEM((z.ext, cols + 128), BF),
                pltpu.VMEM((z.gi * 40, 384), F32),
                pltpu.VMEM((cells, 256), BF),
                pltpu.VMEM((4, cells, 4 * n1), BF),
                pltpu.VMEM((cells, 4 * n2), BF),
                pltpu.VMEM((cells, n3), BF),
                pltpu.VMEM((cells, z.slots * w_squeeze.shape[0]), BF),
                pltpu.VMEM((cells, 3 * n3), BF),
                pltpu.VMEM((2, cells, 4 * n2), BF),
                pltpu.VMEM((4, cells, 6 * n1), BF),
                pltpu.VMEM((4, cells, 6 * n1), BF),
                pltpu.VMEM((rows // 4 * 24, 2 * z.step), F32),
                pltpu.VMEM((cells, 128), F32),
                pltpu.VMEM((cells, 128), F32),
                pltpu.VMEM((cells, 128), F32),
            ],
            compiler_params=pltpu.CompilerParams(vmem_limit_bytes=48 * 2**20),
            name="net",
        )(*operands)

    copied = P()
    in_specs = (
        P("plane", None, "height", "span"),
        P(AXES, None, None, None, None),
    ) + (copied,) * 15
    out_specs = (P("plane", None, "height", "span"), P("plane", None, "height", "span"))
    return jax.shard_map(shards, mesh=mesh, in_specs=in_specs, out_specs=out_specs, check_vma=False)
```

profile of v0, /device:TPU:0, one launch (start us, length us, event | category | flops | bytes accessed | tf_op | source)
XLA Modules:
  0.0 62.7 jit_solution(12484434620440436966)
XLA Ops:
  0.7 1.0 %copy-done.7 = bf16[3,64,512]{2,1,0:T(8,128)(2,1)S(1)} copy-done((bf16[3,64,512]{2,1,0:T(8,128)(2,1)S(1)}, bf16[3,64,512]{2,1,0:T(8,128)(2,1)}, u32[]{:S(2)}) %copy-start.7) | copy-done | bytes 196632
  1.6 0.8 %copy-done.10 = bf16[1,2,3,32,64]{4,3,2,1,0:T(8,128)(2,1)S(1)} copy-done((bf16[1,2,3,32,64]{4,3,2,1,0:T(8,128)(2,1)S(1)}, bf16[1,2,3,32,64]{4,3,2,1,0:T(8,128)(2,1)}, u32[]{:S(2)}) %copy-start.10) | copy-done | bytes 24600
  2.4 0.7 %copy-done.11 = bf16[32,128]{1,0:T(8,128)(2,1)S(1)} copy-done((bf16[32,128]{1,0:T(8,128)(2,1)S(1)}, bf16[32,128]{1,0:T(8,128)(2,1)}, u32[]{:S(2)}) %copy-start.11) | copy-done | bytes 8216
  3.1 0.8 %copy-done.13 = bf16[64,192]{1,0:T(8,128)(2,1)S(1)} copy-done((bf16[64,192]{1,0:T(8,128)(2,1)S(1)}, bf16[64,192]{1,0:T(8,128)(2,1)}, u32[]{:S(2)}) %copy-start.13) | copy-done | bytes 24600
  3.9 2.0 %pack.1 = bf16[32,48,128]{2,1,0:T(8,128)(2,1)} custom-call(bf16[1,3,64,128]{3,2,1,0:T(8,128)(2,1)} %refs_2_.2, bf16[1,2,3,32,64]{4,3,2,1,0:T(8,128)(2,1)S(1)} %copy-done.10, bf16[64,192]{1,0:T(8,128)(2,1)S(1)} %copy-done.13, bf16[32,128]{1,0:T(8,128)(2,1)S(1)} %copy-done.11, bf16[3,64,512]{2,1,0:T(8,128)(2,1)S(1)} %copy-done.7), custom_call_target="tpu_custom_call" | custom-call | tf_op jit(solution)/shard_map/pack/pallas_call | solution.py:481
  5.9 7.3 %all-to-all-start = ((bf16[32,48,128]{2,1,0:T(8,128)(2,1)}), bf16[32,48,128]{2,1,0:T(8,128)(2,1)S(1)}, u32[]{:S(2)}, u32[]{:S(2)}) async-start(bf16[32,48,128]{2,1,0:T(8,128)(2,1)} %pack.1), calls=%async_computation | async-start | bytes 786432 | tf_op jit(solution)/shard_map/all_to_all | solution.py:492
  13.2 1.8 %collective-permute-start = (bf16[3,64,128]{2,1,0:T(8,128)(2,1)}, bf16[3,64,128]{2,1,0:T(8,128)(2,1)}, u32[]{:S(2)}, u32[]{:S(2)}) collective-permute-start(bf16[3,64,128]{2,1,0:T(8,128)(2,1)} %bitcast.3), channel_id=1, source_target_pairs={{0,16},{16,0},{1,17},{17,1},{2,18},{18,2},{3,19},{19,3},{4,20},{20... | collective-permute-start | bytes 147464 | tf_op jit(solution)/shard_map/ppermute | solution.py:497
  15.5 1.0 %copy-done.14 = bf16[6,6,6,16,64]{4,2,1,0,3:T(8,128)(2,1)} copy-done((bf16[6,6,6,16,64]{4,2,1,0,3:T(8,128)(2,1)}, bf16[6,6,6,16,64]{4,2,1,0,3:T(8,128)(2,1)S(1)}, u32[]{:S(2)}) %copy-start.14) | copy-done | bytes 442392
  18.1 0.2 copy.92
  18.8 0.2 fusion.10.refs_21_
  19.4 0.5 fusion.20.refs_5_
  19.9 1.6 %copy.82 = bf16[6,6,6,16,64]{4,3,1,2,0:T(8,128)(2,1)S(1)} copy(bf16[6,6,6,16,64]{4,2,1,0,3:T(8,128)(2,1)} %copy-done.14) | data formatting | bytes 884736 | tf_op jit(solution)/shard_map/stack | solution.py:422
  21.6 1.3 %reshape.42 = bf16[6,3,2,6,1024]{4,2,1,3,0:T(2,128)(2,1)} reshape(bf16[6,6,6,16,64]{4,3,1,2,0:T(8,128)(2,1)S(1)} %copy.82) | data formatting | bytes 884736 | tf_op jit(solution)/shard_map/reshape | solution.py:423
  22.9 1.3 %copy.83 = bf16[2,3,6,6,1024]{4,0,3,2,1:T(2,128)(2,1)S(1)} copy(bf16[2,3,6,6,1024]{4,0,1,2,3:T(2,128)(2,1)} %bitcast.103) | data formatting | bytes 884736 | tf_op jit(solution)/shard_map/transpose | solution.py:423
  24.2 0.4 pad.148
  24.7 0.3 concatenate.19
  25.1 0.9 %copy.94 = bf16[6,256,24]{2,1,0:T(8,128)(2,1)} copy(bf16[6,256,24]{1,2,0:T(8,128)(2,1)S(1)} %concatenate.19) | data formatting | bytes 147456 | tf_op jit(solution)/shard_map/concatenate | solution.py:452
  26.0 1.1 %pad.164.refs_22_ = bf16[6,256,128]{2,1,0:T(8,128)(2,1)S(1)} pad(bf16[6,256,24]{2,1,0:T(8,128)(2,1)} %copy.94, bf16[]{:T(256)} %constant.52.clone.1), padding=0_0x0_0x0_104 | pad | bytes 466946 | tf_op jit(solution)/shard_map/jit(_pad)/pad | solution.py:460
  27.1 2.4 %copy.90 = bf16[3,256,768]{1,2,0:T(8,128)(2,1)} copy(bf16[3,256,768]{2,1,0:T(8,128)(2,1)} %param.37) | data formatting | bytes 2359296 | tf_op args[11]
  29.4 1.1 %copy.85 = bf16[4,128,256]{2,1,0:T(8,128)(2,1)S(1)} copy(bf16[4,128,256]{1,2,0:T(8,128)(2,1)} %bitcast.106) | data formatting | bytes 524288 | tf_op jit(solution)/shard_map/transpose | solution.py:427
  30.6 1.8 %copy.96.refs_18_ = bf16[256,512]{1,0:T(8,128)(2,1)} copy(bf16[256,512]{0,1:T(8,128)(2,1)} %bitcast.107) | data formatting | bytes 524288 | tf_op jit(solution)/shard_map/reshape | solution.py:436
  32.4 0.9 %copy.86 = bf16[128,256]{0,1:T(8,128)(2,1)S(1)} copy(bf16[128,256]{1,0:T(8,128)(2,1)} %param.35) | data formatting | bytes 131072 | tf_op args[9]
  33.3 1.6 %copy.95.refs_20_ = bf16[128,256]{1,0:T(8,128)(2,1)} copy(bf16[128,256]{0,1:T(8,128)(2,1)} %bitcast.109) | data formatting | bytes 131072 | tf_op jit(solution)/shard_map/reshape | solution.py:441
  35.6 0.9 %copy-done.1 = bf16[256,512]{1,0:T(8,128)(2,1)S(1)} copy-done((bf16[256,512]{1,0:T(8,128)(2,1)S(1)}, bf16[256,512]{1,0:T(8,128)(2,1)}, u32[]{:S(2)}) %copy-start.1) | copy-done | bytes 262168
  36.5 1.1 %copy-done.2 = bf16[800,304]{1,0:T(8,128)(2,1)S(1)} copy-done((bf16[800,304]{1,0:T(8,128)(2,1)S(1)}, bf16[800,304]{1,0:T(8,128)(2,1)}, u32[]{:S(2)}) %copy-start.2) | copy-done | bytes 486424
  37.6 1.1 %copy-done.3 = bf16[768,384]{1,0:T(8,128)(2,1)S(1)} copy-done((bf16[768,384]{1,0:T(8,128)(2,1)S(1)}, bf16[768,384]{1,0:T(8,128)(2,1)}, u32[]{:S(2)}) %copy-start.3) | copy-done | bytes 589848
  38.7 1.0 %copy-done.4 = bf16[2,192,384]{2,1,0:T(8,128)(2,1)S(1)} copy-done((bf16[2,192,384]{2,1,0:T(8,128)(2,1)S(1)}, bf16[2,192,384]{2,1,0:T(8,128)(2,1)}, u32[]{:S(2)}) %copy-start.4) | copy-done | bytes 294936
  39.6 0.8 %copy-done.5 = bf16[128,256]{1,0:T(8,128)(2,1)S(1)} copy-done((bf16[128,256]{1,0:T(8,128)(2,1)S(1)}, bf16[128,256]{1,0:T(8,128)(2,1)}, u32[]{:S(2)}) %copy-start.5) | copy-done | bytes 65560
  40.5 0.9 %copy-done.6 = bf16[256,384]{1,0:T(8,128)(2,1)S(1)} copy-done((bf16[256,384]{1,0:T(8,128)(2,1)S(1)}, bf16[256,384]{1,0:T(8,128)(2,1)}, u32[]{:S(2)}) %copy-start.6) | copy-done | bytes 196632
  41.4 0.8 %copy-done.8 = bf16[4,128,64]{1,2,0:T(8,128)(2,1)S(1)} copy-done((bf16[4,128,64]{1,2,0:T(8,128)(2,1)S(1)}, bf16[4,128,64]{1,2,0:T(8,128)(2,1)}, u32[]{:S(2)}) %copy-start.8) | copy-done | bytes 65560
  42.2 0.8 %copy-done.9 = bf16[96,256]{1,0:T(8,128)(2,1)S(1)} copy-done((bf16[96,256]{1,0:T(8,128)(2,1)S(1)}, bf16[96,256]{1,0:T(8,128)(2,1)}, u32[]{:S(2)}) %copy-start.9) | copy-done | bytes 49176
  43.0 19.7 %net.1 = (bf16[1,3,64,128]{3,2,1,0:T(8,128)(2,1)}, f32[1,3,64,128]{3,2,1,0:T(8,128)}) custom-call(s32[1]{0:T(128)S(6)} %copy.116.refs_0_, f32[4]{0:T(128)S(1)} %pad_maximum_fusion.1.refs_1_, bf16[1,3,64,128]{3,2,1,0:T(8,128)(2,1)} %refs_2_.2, bf16[1,3,64,128]{3,2,1,0:T(8,128)(2,1)} %bitcast.4.refs_3_, bf16[32,48,128]{2,1,0:T(8,128)(2,1)S(1)} %all-to-all-done.refs_4_, ...), custom_call_target="tpu_custom_call" | custom-call | tf_op jit(solution)/shard_map/net/pallas_call | solution.py:517
  (63 shorter events, 2.0 us)
Async XLA Ops:
  0.6 18.8 %copy-start = (f32[256,448]{0,1:T(8,128)S(1)}, f32[256,448]{0,1:T(8,128)}, u32[]{:S(2)}) copy-start(f32[256,448]{0,1:T(8,128)} %param.31) | copy-start | bytes 1376260
  0.6 1.0 %copy-start.7 = (bf16[3,64,512]{2,1,0:T(8,128)(2,1)S(1)}, bf16[3,64,512]{2,1,0:T(8,128)(2,1)}, u32[]{:S(2)}) copy-start(bf16[3,64,512]{2,1,0:T(8,128)(2,1)} %constant.58.clone.refs_4_) | copy-start | bytes 589828
  1.6 0.8 %copy-start.10 = (bf16[1,2,3,32,64]{4,3,2,1,0:T(8,128)(2,1)S(1)}, bf16[1,2,3,32,64]{4,3,2,1,0:T(8,128)(2,1)}, u32[]{:S(2)}) copy-start(bf16[1,2,3,32,64]{4,3,2,1,0:T(8,128)(2,1)} %refs_1_.1) | copy-start | bytes 73732
  2.4 0.7 %copy-start.11 = (bf16[32,128]{1,0:T(8,128)(2,1)S(1)}, bf16[32,128]{1,0:T(8,128)(2,1)}, u32[]{:S(2)}) copy-start(bf16[32,128]{1,0:T(8,128)(2,1)} %constant.57.clone.refs_3_.refs_9_) | copy-start | bytes 24580
  3.1 0.8 %copy-start.13 = (bf16[64,192]{1,0:T(8,128)(2,1)S(1)}, bf16[64,192]{1,0:T(8,128)(2,1)}, u32[]{:S(2)}) copy-start(bf16[64,192]{1,0:T(8,128)(2,1)} %constant.56.clone.refs_2_) | copy-start | bytes 73732
  3.9 11.2 %copy-start.19 = (bf16[3,64,18]{1,2,0:T(8,128)(2,1)S(1)}, bf16[3,64,18]{1,2,0:T(8,128)(2,1)}, u32[]{:S(2)}) copy-start(bf16[3,64,18]{1,2,0:T(8,128)(2,1)} %param.32) | copy-start | bytes 20740
  5.9 10.6 %copy-start.20 = (bf16[3,3,192]{2,1,0:T(4,128)(2,1)S(1)}, bf16[3,3,192]{2,1,0:T(4,128)(2,1)}, u32[]{:S(2)}) copy-start(bf16[3,3,192]{2,1,0:T(4,128)(2,1)} %param.42) | copy-start | bytes 10372
  5.9 11.8 %copy-start.16 = (bf16[3,256,128]{2,1,0:T(8,128)(2,1)S(1)}, bf16[3,256,128]{2,1,0:T(8,128)(2,1)}, u32[]{:S(2)}) copy-start(bf16[3,256,128]{2,1,0:T(8,128)(2,1)} %param.36) | copy-start | bytes 589828
  5.9 29.7 %all-to-all-start = ((bf16[32,48,128]{2,1,0:T(8,128)(2,1)}), bf16[32,48,128]{2,1,0:T(8,128)(2,1)S(1)}, u32[]{:S(2)}, u32[]{:S(2)}) async-start(bf16[32,48,128]{2,1,0:T(8,128)(2,1)} %pack.1), calls=%async_computation | async-start | bytes 786432 | tf_op jit(solution)/shard_map/all_to_all | solution.py:492
  13.2 22.3 %collective-permute-start = (bf16[3,64,128]{2,1,0:T(8,128)(2,1)}, bf16[3,64,128]{2,1,0:T(8,128)(2,1)}, u32[]{:S(2)}, u32[]{:S(2)}) collective-permute-start(bf16[3,64,128]{2,1,0:T(8,128)(2,1)} %bitcast.3), channel_id=1, source_target_pairs={{0,16},{16,0},{1,17},{17,1},{2,18},{18,2},{3,19},{19,3},{4,20},{20... | collective-permute-start | bytes 147464 | tf_op jit(solution)/shard_map/ppermute | solution.py:497
  15.1 3.0 %copy-start.15 = (bf16[3,128,384]{2,1,0:T(8,128)(2,1)S(1)}, bf16[3,128,384]{2,1,0:T(8,128)(2,1)}, u32[]{:S(2)}) copy-start(bf16[3,128,384]{2,1,0:T(8,128)(2,1)} %param.39) | copy-start | bytes 884740
  15.5 1.1 %copy-start.14 = (bf16[6,6,6,16,64]{4,2,1,0,3:T(8,128)(2,1)}, bf16[6,6,6,16,64]{4,2,1,0,3:T(8,128)(2,1)S(1)}, u32[]{:S(2)}) copy-start(bf16[6,6,6,16,64]{4,2,1,0,3:T(8,128)(2,1)S(1)} %bitcast_dynamic-update-slice_fusion) | copy-start | bytes 1327108
  17.7 0.9 %copy-start.17 = (bf16[3,64,192]{2,1,0:T(8,128)(2,1)S(1)}, bf16[3,64,192]{2,1,0:T(8,128)(2,1)}, u32[]{:S(2)}) copy-start(bf16[3,64,192]{2,1,0:T(8,128)(2,1)} %param.41) | copy-start | bytes 221188
  18.3 0.9 %copy-start.18 = (f32[64,256]{1,0:T(8,128)S(1)}, f32[64,256]{1,0:T(8,128)}, u32[]{:S(2)}) copy-start(f32[64,256]{1,0:T(8,128)} %param.30) | copy-start | bytes 196612
  29.4 6.1 %copy-start.12 = (bf16[32,128]{1,0:T(8,128)(2,1)S(1)}, bf16[32,128]{1,0:T(8,128)(2,1)}, u32[]{:S(2)}) copy-start(bf16[32,128]{1,0:T(8,128)(2,1)} %constant.57.clone.refs_3_.refs_9_) | copy-start | bytes 24580
  35.6 1.0 %copy-start.1 = (bf16[256,512]{1,0:T(8,128)(2,1)S(1)}, bf16[256,512]{1,0:T(8,128)(2,1)}, u32[]{:S(2)}) copy-start(bf16[256,512]{1,0:T(8,128)(2,1)} %copy.96.refs_18_) | copy-start | bytes 786436
  36.5 1.1 %copy-start.2 = (bf16[800,304]{1,0:T(8,128)(2,1)S(1)}, bf16[800,304]{1,0:T(8,128)(2,1)}, u32[]{:S(2)}) copy-start(bf16[800,304]{1,0:T(8,128)(2,1)} %constant.61.clone.refs_8_) | copy-start | bytes 1459204
  37.6 1.1 %copy-start.3 = (bf16[768,384]{1,0:T(8,128)(2,1)S(1)}, bf16[768,384]{1,0:T(8,128)(2,1)}, u32[]{:S(2)}) copy-start(bf16[768,384]{1,0:T(8,128)(2,1)} %constant.60.clone.refs_7_) | copy-start | bytes 1769476
  38.7 1.0 %copy-start.4 = (bf16[2,192,384]{2,1,0:T(8,128)(2,1)S(1)}, bf16[2,192,384]{2,1,0:T(8,128)(2,1)}, u32[]{:S(2)}) copy-start(bf16[2,192,384]{2,1,0:T(8,128)(2,1)} %constant.63.clone.refs_11_) | copy-start | bytes 884740
  39.6 0.8 %copy-start.5 = (bf16[128,256]{1,0:T(8,128)(2,1)S(1)}, bf16[128,256]{1,0:T(8,128)(2,1)}, u32[]{:S(2)}) copy-start(bf16[128,256]{1,0:T(8,128)(2,1)} %copy.95.refs_20_) | copy-start | bytes 196612
  40.5 0.9 %copy-start.6 = (bf16[256,384]{1,0:T(8,128)(2,1)S(1)}, bf16[256,384]{1,0:T(8,128)(2,1)}, u32[]{:S(2)}) copy-start(bf16[256,384]{1,0:T(8,128)(2,1)} %constant.59.clone.refs_6_) | copy-start | bytes 589828
  41.4 0.8 %copy-start.8 = (bf16[4,128,64]{1,2,0:T(8,128)(2,1)S(1)}, bf16[4,128,64]{1,2,0:T(8,128)(2,1)}, u32[]{:S(2)}) copy-start(bf16[4,128,64]{1,2,0:T(8,128)(2,1)} %param.33) | copy-start | bytes 196612
  42.2 0.8 %copy-start.9 = (bf16[96,256]{1,0:T(8,128)(2,1)S(1)}, bf16[96,256]{1,0:T(8,128)(2,1)}, u32[]{:S(2)}) copy-start(bf16[96,256]{1,0:T(8,128)(2,1)} %constant.62.clone.refs_10_) | copy-start | bytes 147460
where the time goes:
time: 63.9 us; the launch traced here: 62.7 us
  local copies, waits for them, and re-layouts  28.2 us (44%)
  Pallas kernels  21.7 us (34%)
  starting transfers between devices  9.13 us (14%)
  between operations  2.58 us (4%)
  matrix products  0.65 us (1%)
    pallas_call x1, Pallas kernels, shards(): pl.pallas_call(lambda *refs: net_kernel(z, *refs), out_shape=(jax.ShapeDt...  19.7 us
    unnamed x64, local copies, waits for them, and re-layouts  16.5 us
    all_to_all x1, starting transfers between devices, shards(): recv = lax.all_to_all(send, AXES, 0, 0, tiled=True)  7.3 us
    pallas_call x1, Pallas kernels, shards(): pl.pallas_call(lambda *refs: pack_kernel(z, *refs), out_shape=jax.ShapeDt...  2.02 us
    ppermute x1, starting transfers between devices, shards(): others = lax.ppermute(tile, 'plane', [(0, 1), (1, 0)])[None]  1.83 us
    reshape x1, local copies, waits for them, and re-layouts, lay_weights(): w_rm = rise_mid.transpose(2, 0, 1).reshape(n3, 4 * n2)  1.82 us
    another operation x2, local copies, waits for them, and re-layouts, lay_weights(): w = jnp.stack(parts, axis=3)  1.67 us
    reshape x1, local copies, waits for them, and re-layouts, lay_weights(): w_rf = rise_fine.transpose(2, 0, 1).reshape(n2, 4 * n1)  1.58 us
  transfers between devices with their start and end apart: 2, of which 0 were waited for; matrix products, arithmetic and copies ran while one was open for 27% of the time, Pallas kernels for 0%

commit v1 on v0

--- a/solution.py
+++ b/solution.py
@@ -48,8 +48,10 @@
         self.strip = up(3 * RIM, 16)
         self.ext = 2 * self.strip + 3 * rows
         self.patch_rows, self.patch_cols = rows // CF + 4, cols // CF + 4
-        self.patch = up(self.patch_rows, 16)
-        self.piece = self.strip + self.patch * ((self.slots + 1) // 2)
+        self.pairs = (self.slots + 1) // 2
+        self.piece = up(3 * RIM + self.patch_rows * self.pairs, 8)
+        self.pad = up(3 * RIM + self.patch_rows * self.pairs, 8)
+        self.patch = up(self.piece, 16)
 
     def planes_of(self, plane):
         if self.planes == 1:
@@ -57,27 +59,6 @@
         if self.planes == 2:
             return [plane, 1 - plane]
         return [plane, plane - 1, plane + 1]
-
-
-def pack_constants(z):
-    bottom = np.zeros((z.strip, 3 * z.rows), np.float32)
-    top = np.zeros((z.strip, 3 * z.rows), np.float32)
-    for c in range(3):
-        for r in range(RIM):
-            bottom[c * RIM + r, c * z.rows + z.rows - RIM + r] = 1
-            top[c * RIM + r, c * z.rows + r] = 1
-    sides = np.zeros((2 * 16, z.cols), np.float32)
-    for r in range(RIM):
-        sides[r, z.cols - RIM + r] = 1
-        sides[16 + r, r] = 1
-    window = np.zeros((3, z.cond_cols, z.spans * 128), np.float32)
-    for s in range(z.spans):
-        for x in range(z.patch_cols):
-            col = s * (z.cols // CF) + x - 2
-            if 0 <= col < z.cond_cols:
-                for c in range(3):
-                    window[c, col, s * 128 + c * z.patch_cols + x] = 1
-    return np.concatenate([bottom, top]).astype(BF), sides.astype(BF), window.astype(BF)
 
 
 def unpack_constants(z):
@@ -95,7 +76,7 @@
             for half in range(2):
                 for c in range(3):
                     lift[half, c, half * 64 + c * z.patch_cols + col // CF + 2, b * 64 + j] = 1
-    down = np.zeros((z.gi * 40, z.ext + 3 * z.patch), np.float32)
+    down = np.zeros((z.pairs, z.gi * 40, z.ext + 3 * z.patch), np.float32)
     for i in range(z.gi):
         for c in range(3):
             for a in range(6):
@@ -106,8 +87,10 @@
                     source = z.strip + c * z.rows + row
                 else:
                     source = z.strip + 3 * z.rows + c * RIM + row - z.rows
-                down[i * 40 + c * 6 + a, source] = 1
-                down[i * 40 + 18 + c * 6 + a, z.ext + c * z.patch + row // CF + 2] = 1
+                down[:, i * 40 + c * 6 + a, source] = 1
+                for pair in range(z.pairs):
+                    at = z.ext + c * z.patch + 3 * RIM + pair * z.patch_rows + row // CF + 2
+                    down[pair, i * 40 + 18 + c * 6 + a, at] = 1
     sides = np.zeros((2 * 16, 128), np.float32)
     for r in range(RIM):
         sides[r, 128 - RIM + r] = 1
@@ -129,38 +112,92 @@
     )
 
 
-def pack_kernel(z, noisy, slot, strips, sides, window, send, padded):
+def fetch(pairs, sems):
+    copies = [
+        pltpu.make_async_copy(source, target, sems.at[n])
+        for n, (source, target) in enumerate(pairs)
+    ]
+    for copy in copies:
+        copy.start()
+    return copies
+
+
+def pack_kernel(z, noisy_hbm, slot_hbm, send, noisy, slot, padded, sems):
+    tile_copy, slot_copy = fetch(((noisy_hbm, noisy), (slot_hbm, slot)), sems)
     plane, span, height = (lax.axis_index(a) for a in AXES)
-    tile = noisy[0].reshape(3 * z.rows, z.cols)
-    ends = dot(strips[...], tile).astype(BF)
-    cols = dot_nt(sides[...], tile).astype(BF)
+    tall, across = z.rows // CF, z.cols // CF
+
+    shape = (z.cond_cols, z.spans * 128)
+    col = lax.broadcasted_iota(jnp.int32, shape, 0)
+    lane = lax.broadcasted_iota(jnp.int32, shape, 1)
+    windows = []
+    for c in range(3):
+        x = (lane & 127) - c * z.patch_cols
+        hit = (x >= 0) & (x < z.patch_cols) & (col == (lane >> 7) * across + x - 2)
+        windows.append(jnp.where(hit, 1.0, 0.0).astype(BF))
+    shape = (2 * z.strip, 3 * z.rows)
+    row = lax.broadcasted_iota(jnp.int32, shape, 0)
+    lane = lax.broadcasted_iota(jnp.int32, shape, 1)
+    strips = jnp.zeros(shape, F32)
+    for half, first in ((0, z.rows - RIM), (z.strip, 0)):
+        for c in range(3):
+            r = row - half - c * RIM
+            hit = (r >= 0) & (r < RIM) & (lane == c * z.rows + first + r)
+            strips = jnp.where(hit, 1.0, strips)
+    strips = strips.astype(BF)
+    shape = (32, z.cols)
+    row = lax.broadcasted_iota(jnp.int32, shape, 0)
+    lane = lax.broadcasted_iota(jnp.int32, shape, 1)
+    hit = (row < RIM) & (lane == z.cols - RIM + row)
+    hit = hit | ((row >= 16) & (row < 16 + RIM) & (lane == row - 16))
+    sides = jnp.where(hit, 1.0, 0.0).astype(BF)
+
+    base = 3 * RIM
+    padded[...] = jnp.zeros_like(padded)
+    slot_copy.wait()
     wide = None
     for c in range(3):
-        part = dot(slot[0, :, c].reshape(z.planes * z.cond_rows, z.cond_cols), window[c])
+        part = dot(slot[0, :, c].reshape(z.planes * z.cond_rows, z.cond_cols), windows[c])
         wide = part if wide is None else wide + part
-    padded[...] = jnp.zeros_like(padded)
     for p in range(z.planes):
-        padded[p, 2 : 2 + z.cond_rows, :] = wide[p * z.cond_rows : (p + 1) * z.cond_rows]
-    send[:, 0 : z.strip, :] = jnp.zeros((z.devices, z.strip, 128), BF)
-    tall = z.rows // CF
+        at = z.pad + 2
+        padded[p, at : at + z.cond_rows, :] = wide[p * z.cond_rows : (p + 1) * z.cond_rows]
+    tile_copy.wait()
+    tile = noisy[0].reshape(3 * z.rows, z.cols)
+    ends = dot(strips, tile)
+    cols = dot_nt(sides, tile)
+
+    rows = lax.broadcasted_iota(jnp.int32, (z.piece, 128), 0)
     for p in range(z.planes):
         for s in range(z.spans):
             for h in range(z.heights):
                 target = (p * z.spans + s) * z.heights + h
+                total = jnp.zeros((z.piece, 128), F32)
                 for k0 in range(0, z.slots, 2):
+                    first = base + k0 // 2 * z.patch_rows
+                    mine = (rows >= first) & (rows < first + z.patch_rows)
                     both = None
                     for k in range(k0, min(k0 + 2, z.slots)):
                         q = z.planes_of(p)[k]
                         if 0 <= q < z.planes:
-                            part = padded[
-                                q, tall * h : tall * h + z.patch, s * 128 : (s + 1) * 128
-                            ]
+                            at = z.pad + tall * h - first
+                            part = padded[q, at : at + z.piece, s * 128 : (s + 1) * 128]
                             part = part if k == k0 else pltpu.roll(part, 64, 1)
                             both = part if both is None else both + part
-                    if both is None:
-                        both = jnp.zeros((z.patch, 128), F32)
-                    base = z.strip + k0 // 2 * z.patch
-                    send[target, base : base + z.patch, :] = both.astype(BF)
+                    if both is not None:
+                        total = jnp.where(mine, both, total)
+                send[target] = total.astype(BF)
+    rest = jnp.zeros((z.piece - z.strip, 128), F32)
+    blank = jnp.zeros((16, 128 - (3 * z.rows) % 128), F32)
+    side = []
+    for half in (0, 16):
+        part = jnp.concatenate([cols[half : half + 16], blank], axis=1)
+        side.append(
+            jnp.concatenate([part[:, 0:128], part[:, 128:256], rest], axis=0)
+        )
+    ends = [
+        jnp.concatenate([ends[half : half + z.strip], rest], axis=0) for half in (0, z.strip)
+    ]
     for k in range(z.slots):
         q = z.planes_of(plane)[k]
         for dh in (-1, 0, 1):
@@ -177,21 +214,22 @@
                 def _(q=q, dh=dh, ds=ds):
                     target = (q * z.spans + span + ds) * z.heights + height + dh
                     if dh != 0:
-                        half = 0 if dh > 0 else z.strip
-                        send[target, 0 : z.strip, :] = ends[half : half + z.strip]
+                        strip = ends[0 if dh > 0 else 1]
                     else:
-                        half = 0 if ds > 0 else 16
-                        send[target, 0:16, :] = cols[half : half + 16, 0:128]
-                        send[target, 16:32, 0:64] = cols[half : half + 16, 128:192]
+                        strip = side[0 if ds > 0 else 1]
+                    send[target] = (send[target].astype(F32) + strip).astype(BF)
 
 
 def net_kernel(
-    z, owner, coefs, noisy, others, recv, bias,
-    across, lift, down, sides, spread, gather,
-    w_in, w_pf, w_pm, w_sq, w_ac, w_mid, w_rm, w_dm, w_rf, w_df, w_lv,
-    pred, sample,
-    ext, grid, entry, h1, d1, d2, sq, mx, v2, v1, e1, last, mask, half, halfp,
+    z, count, owner, noisy, others, recv, bias, *refs
 ):
+    far, refs = refs[:count], refs[count:]
+    pred, sample, refs = refs[0], refs[1], refs[2:]
+    near, refs = refs[:count], refs[count:]
+    ext, grid, entry, h1, d1, d2, sq, mx, v2, v1, e1, last, mask, half, halfp, sems = refs
+    copies = fetch(tuple(zip(far, near)), sems)
+    across, lift, down, sides, spread, gather = near[:6]
+    w_in, w_pf, w_pm, w_sq, w_ac, w_mid, w_rm, w_dm, w_rf, w_df, w_lv = near[6:]
     plane, span, height = (lax.axis_index(a) for a in AXES)
     step, gi = z.step, z.gi
     n1, n2, n3 = w_in.shape[1] // 16, w_pf.shape[1], w_pm.shape[1]
@@ -220,6 +258,8 @@
     b2 = bias[:, n1 : n1 + n2]
     b3 = bias[:, n1 + n2 : n1 + n2 + n3]
 
+    for copy in copies[:4]:
+        copy.wait()
     for k in range(z.slots):
         q = z.planes_of(plane)[k]
 
@@ -231,7 +271,7 @@
             )
             source = (q * z.spans + span + ds) * z.heights + height + dh
             source = jnp.clip(source, 0, z.devices - 1)
-            value = recv[source, 0 : z.strip, :].astype(F32)
+            value = recv[source].astype(F32)[0 : z.strip]
             return jnp.where(ok, value, 0.0)
 
         tile = (noisy[0] if k == 0 else others[k - 1]).reshape(3 * z.rows, z.cols)
@@ -250,13 +290,14 @@
         ext[z.strip : z.strip + 3 * z.rows, z.cols : z.cols + 128] = dot(
             rims, sides[...]
         ).astype(BF)
-        base = z.strip + k // 2 * z.patch
-        patch = recv[owner[0], base : base + z.patch, :]
+        patch = recv[owner[0]].astype(F32)
+        patch = jnp.concatenate([patch, jnp.zeros((z.patch - z.piece, 128), F32)], axis=0)
+        patch = patch.astype(BF)
         wide_rows = [dot(ext[...], across[...]).astype(BF)]
         for c in range(3):
             at = (k % 2 * 3 + c) * 128
             wide_rows.append(dot(patch, lift[at : at + 128, :]).astype(BF))
-        grid[...] = dot(down[...], jnp.concatenate(wide_rows, axis=0))
+        grid[...] = dot(down[k // 2], jnp.concatenate(wide_rows, axis=0))
         for i in range(gi):
             block = grid[i * 40 : (i + 1) * 40, :]
             stack = jnp.concatenate(
@@ -267,6 +308,9 @@
             at = i * step
             entry[at : at + step, 0:128] = turned[0:step].astype(BF)
             entry[at : at + step, 128:256] = turned[64 : 64 + step].astype(BF)
+        if k == 0:
+            for copy in copies[6:10]:
+                copy.wait()
         per = 5 if gi % 5 == 0 else 1
         for i in range(0, gi, per):
             rows = slice(i * step, (i + per) * step)
@@ -297,6 +341,8 @@
     def span_of(i, n, shift=0):
         return slice((i + shift) * step, (i + shift + n) * step)
 
+    for copy in copies[4:6] + copies[10:]:
+        copy.wait()
     for i, n in chunks(0, gi, 5):
         rows = span_of(i, n)
         m = d2[rows, :].astype(F32) + dot(sq[rows, :], w_ac[...])
@@ -387,8 +433,9 @@
     guess = guess + dot(gather[1], spread_out[:, z.cols :])
     pred[0] = guess.astype(BF).reshape(3, z.rows, z.cols)
     given = noisy[0].reshape(3 * z.rows, z.cols).astype(F32)
-    clean = (given - coefs[0] * guess) * coefs[1]
-    result = coefs[2] * clean + coefs[3] * guess
+    at = n1 + n2 + n3
+    back, rise, keep, add = (bias[:, at + t : at + t + 1] for t in range(4))
+    result = keep * ((given - back * guess) * rise) + add * guess
     sample[0] = result.reshape(3, z.rows, z.cols)
 
 
@@ -406,63 +453,101 @@
     return jnp.dot(hidden, w_biases, precision=lax.Precision.HIGHEST)
 
 
-def lay_weights(
-    z, plane, w_enter, pool_fine, pool_mid, w_squeeze, w_across, w_middle,
-    rise_mid, decode_mid, rise_fine, decode_fine, w_leave,
-):
-    n1, n2, n3 = w_enter.shape[1], pool_fine.shape[1], pool_mid.shape[1]
-    w = w_enter.reshape(3, n1, 3, 6).transpose(0, 2, 3, 1)
-    parts = []
-    for p in range(2):
-        for q in range(2):
-            for a in range(2):
-                for b in range(2):
-                    y, x = 2 * p + a, 2 * q + b
-                    parts.append(jnp.pad(w, ((y, 3 - y), (x, 3 - x), (0, 0), (0, 0))))
-    w = jnp.stack(parts, axis=3)
-    w = w.reshape(6, 3, 2, 6, 16 * n1).transpose(2, 1, 3, 0, 4).reshape(2, 3, 36, 16 * n1)
-    w = jnp.pad(w, ((0, 0), (0, 0), (0, 4), (0, 0))).reshape(2, 120, 16 * n1)
-    w_in = jnp.pad(w, ((0, 0), (0, 8), (0, 0))).reshape(256, 16 * n1)
-    w_pf = pool_fine.transpose(0, 2, 1).reshape(4 * n1, n2)
-    w_pm = pool_mid.transpose(0, 2, 1).reshape(4 * n2, n3)
+def entry_constants():
+    place = np.zeros((8, 256, 128), np.float32)
+    for y in range(4):
+        for pair in range(2):
+            for h in range(2):
+                for la in range(3):
+                    for lb in range(3):
+                        for cin in range(6):
+                            a, b = y + la, 2 * pair + h + lb
+                            row = b % 2 * 128 + b // 2 * 40 + cin * 6 + a
+                            place[y * 2 + pair, row, h * 64 + la * 18 + lb * 6 + cin] = 1
+    return place.astype(BF)
+
+
+def lay_kernel(z, count, *refs):
+    far, refs = refs[:count], refs[count:]
+    tile, refs = refs[0], refs[1:]
+    w_in, w_pm, w_sq, w_ac, w_mid, w_rm, w_dm, w_rf, w_df, w_lv = refs[:10]
+    near, refs = refs[10 : 10 + count], refs[10 + count :]
+    nat, tall, leave, enter, sems = refs
+    copies = fetch(tuple(zip(far, near)), sems)
+    (noisy, place, w_enter, w_leave, pool_mid, w_squeeze, w_across, w_middle,
+     rise_mid, decode_mid, rise_fine, decode_fine) = near
+    plane = lax.axis_index("plane")
+    n1, n2, n3 = decode_fine.shape[1], decode_mid.shape[1], w_middle.shape[1]
+
+    for copy in copies:
+        copy.wait()
+    tile[...] = noisy[0]
+    tall[...] = jnp.zeros_like(tall)
+    leave[...] = jnp.zeros_like(leave)
+    enter[...] = jnp.zeros_like(enter)
+    blank = jnp.zeros(w_enter.shape[1:], F32)
+    for a in range(3):
+        leave[3 * a : 3 * a + 3, 0 : 3 * n1] = w_leave[a].astype(F32)
+        for h in range(2):
+            taps = w_enter[a].astype(F32)
+            taps = jnp.concatenate([blank, taps] if h else [taps, blank], axis=1)
+            enter[h * n1 + a * 18 : h * n1 + a * 18 + 18, :] = taps
+    turned = jnp.transpose(leave[...])[0 : 3 * n1].astype(BF)
+    spots = enter[...].astype(BF)
+    for b in range(2):
+        tall[b, b * n1 : (b + 3) * n1, :] = turned
+    line = lax.broadcasted_iota(jnp.int32, (128, 128), 0)
+    lane = lax.broadcasted_iota(jnp.int32, (128, 128), 1)
+    for y in range(6):
+        total = None
+        for b in range(2):
+            pick = jnp.zeros((128, 128), F32)
+            for a in range(4):
+                if 0 <= y - a < 3:
+                    o = lane - (6 * a + 3 * b)
+                    hit = (o >= 0) & (o < 3) & (line == 3 * (y - a) + o)
+                    pick = jnp.where(hit, 1.0, pick)
+            part = dot(tall[b], pick.astype(BF))
+            total = part if total is None else total + part
+        w_lv[y] = total.astype(BF)
+
+    for y in range(4):
+        for pair in range(2):
+            at = ((y // 2 * 2 + pair) * 2 + y % 2) * 2 * n1
+            w_in[:, at : at + 2 * n1] = dot(place[y * 2 + pair], spots).astype(BF)
+    for t in range(4):
+        w_pm[t * n2 : (t + 1) * n2, :] = jnp.transpose(pool_mid[t])
+        w_rm[:, t * n2 : (t + 1) * n2] = jnp.transpose(rise_mid[t])
+    w_sq[...] = jnp.transpose(w_squeeze[...])
+    width = w_across.shape[2]
     taps = [w_across[1]]
+    zero = jnp.zeros_like(taps[0])
     if z.planes == 2:
         taps.append(jnp.where(plane == 0, w_across[2], w_across[0]))
     elif z.planes > 2:
-        taps.append(jnp.where(plane > 0, w_across[0], jnp.zeros_like(w_across[0])))
-        taps.append(jnp.where(plane < z.planes - 1, w_across[2], jnp.zeros_like(w_across[2])))
-    w_ac = jnp.concatenate([t.T for t in taps], axis=0)
-    w_mid = w_middle.transpose(0, 2, 1)
-    w_rm = rise_mid.transpose(2, 0, 1).reshape(n3, 4 * n2)
-    w = decode_mid.transpose(0, 2, 1)
-    w_dm = jnp.concatenate(
-        [jnp.pad(w, ((0, 0), (q * n2, (1 - q) * n2), (0, 0))) for q in range(2)], axis=2
-    )
-    w_rf = rise_fine.transpose(2, 0, 1).reshape(n2, 4 * n1)
-    w = decode_fine.transpose(0, 2, 1)
-    w_df = jnp.concatenate(
-        [
-            jnp.pad(w, ((a, 1 - a), (b * n1, (1 - b) * n1), (0, 0)))
-            for a in range(2)
-            for b in range(2)
-        ],
-        axis=2,
-    )
-    w = w_leave.transpose(0, 2, 1)
-    w_lv = jnp.concatenate(
-        [
-            jnp.pad(w, ((a, 3 - a), (b * n1, (1 - b) * n1), (0, 0)))
-            for a in range(4)
-            for b in range(2)
-        ],
-        axis=2,
-    )
-    w_lv = jnp.pad(w_lv, ((0, 0), (0, 0), (0, 128 - w_lv.shape[2])))
-    return w_in, w_pf, w_pm, w_sq_t(w_squeeze), w_ac, w_mid, w_rm, w_dm, w_rf, w_df, w_lv
-
-
-def w_sq_t(w_squeeze):
-    return w_squeeze.T
+        taps.append(jnp.where(plane > 0, w_across[0], zero))
+        taps.append(jnp.where(plane < z.planes - 1, w_across[2], zero))
+    for k, tap in enumerate(taps):
+        w_ac[k * width : (k + 1) * width, :] = jnp.transpose(tap)
+    for a in range(3):
+        w_mid[a] = jnp.transpose(w_middle[a])
+        turned = jnp.transpose(decode_mid[a])
+        w_dm[a] = jnp.zeros((4 * n2, 2 * n2), BF)
+        w_dm[a, 0 : 3 * n2, 0:n2] = turned
+        w_dm[a, n2 : 4 * n2, n2 : 2 * n2] = turned
+    w_rf[...] = jnp.transpose(rise_fine[...].reshape(4 * n1, n2))
+
+    nat[...] = jnp.zeros_like(nat)
+    for a in range(3):
+        for b in range(2):
+            wide = jnp.concatenate(
+                [decode_fine[a].astype(F32), jnp.zeros((n1, n1), F32)], axis=1
+            )
+            wide = pltpu.roll(wide, b * n1, 1) if b else wide
+            for r in range(2):
+                nat[a + r, (2 * r + b) * n1 : (2 * r + b + 1) * n1, :] = wide.astype(BF)
+    for a in range(4):
+        w_df[a] = jnp.transpose(nat[a])
 
 
 def solution(mesh):
@@ -477,20 +562,57 @@
         n1, n2, n3 = w_enter.shape[1], pool_fine.shape[1], pool_mid.shape[1]
         vmem = pl.BlockSpec(memory_space=pltpu.VMEM)
         smem = pl.BlockSpec(memory_space=pltpu.SMEM)
-        strips, sides, window = (jnp.asarray(m) for m in pack_constants(z))
+        far = pl.BlockSpec(memory_space=pltpu.HBM)
         send = pl.pallas_call(
             lambda *refs: pack_kernel(z, *refs),
             out_shape=jax.ShapeDtypeStruct((z.devices, z.piece, 128), BF),
-            in_specs=[vmem] * 5,
+            in_specs=[far] * 2,
             out_specs=vmem,
             scratch_shapes=[
-                pltpu.VMEM((planes, up(z.cond_rows + 4 + 8, 8), spans * 128), F32)
+                pltpu.VMEM(noisy.shape, BF),
+                pltpu.VMEM(coarse_cond.shape, BF),
+                pltpu.VMEM((planes, up(z.cond_rows, 8) + 2 * z.pad, spans * 128), F32),
+                pltpu.SemaphoreType.DMA((2,)),
             ],
-            compiler_params=pltpu.CompilerParams(vmem_limit_bytes=32 * 2**20),
+            compiler_params=pltpu.CompilerParams(vmem_limit_bytes=63 * 2**20),
             name="pack",
-        )(noisy, coarse_cond, strips, sides, window)
+        )(noisy, coarse_cond)
         recv = lax.all_to_all(send, AXES, 0, 0, tiled=True)
-        tile = noisy[0]
+        now, prior = plan(timestep[0]), plan(timestep[0] - STRIDE)
+        coefs = jnp.stack(
+            [jnp.sqrt(1.0 - now), 1.0 / jnp.sqrt(now), jnp.sqrt(prior), jnp.sqrt(1.0 - prior)]
+        )
+        bias = jnp.concatenate([time_bias(timestep, w_embed, w_biases), coefs])[None]
+        raw = (
+            noisy, jnp.asarray(entry_constants()), w_enter.transpose(0, 2, 1), w_leave, pool_mid,
+            w_squeeze, w_across, w_middle, rise_mid, decode_mid, rise_fine, decode_fine,
+        )
+        inner = w_squeeze.shape[0]
+        shapes = (
+            noisy.shape[1:],
+            (256, 16 * n1), (4 * n2, n3), (n3, inner), (z.slots * inner, n3),
+            (3, 3 * n3, n3), (n3, 4 * n2), (3, 4 * n2, 2 * n2), (n2, 4 * n1),
+            (4, 4 * n1, 4 * n1), (6, 4 * n1, 128),
+        )
+        tile, *weights = pl.pallas_call(
+            lambda *refs: lay_kernel(z, len(raw), *refs),
+            out_shape=tuple(jax.ShapeDtypeStruct(shape, BF) for shape in shapes),
+            in_specs=[far] * len(raw),
+            out_specs=(vmem,) * len(shapes),
+            scratch_shapes=[pltpu.VMEM(w.shape, BF) for w in raw]
+            + [
+                pltpu.VMEM((4, 4 * n1, 4 * n1), BF),
+                pltpu.VMEM((2, 4 * n1, 128), BF),
+                pltpu.VMEM((128, 4 * n1), F32),
+                pltpu.VMEM((2 * n1, 2 * n1), F32),
+                pltpu.SemaphoreType.DMA((len(raw),)),
+            ],
+            compiler_params=pltpu.CompilerParams(vmem_limit_bytes=63 * 2**20),
+            cost_estimate=pl.CostEstimate(
+                flops=10**9, bytes_accessed=10**7, transcendentals=0
+            ),
+            name="lay",
+        )(*raw)
         if planes == 1:
             others = tile[None]
         elif planes == 2:
@@ -501,35 +623,27 @@
             others = jnp.stack(
                 [lax.ppermute(tile, "plane", ahead), lax.ppermute(tile, "plane", behind)]
             )
-        plane = lax.axis_index("plane")
-        bias = time_bias(timestep, w_embed, w_biases)[None]
-        now, prior = plan(timestep[0]), plan(timestep[0] - STRIDE)
-        coefs = jnp.stack(
-            [jnp.sqrt(1.0 - now), 1.0 / jnp.sqrt(now), jnp.sqrt(prior), jnp.sqrt(1.0 - prior)]
-        )
-        weights = lay_weights(
-            z, plane, w_enter, pool_fine, pool_mid, w_squeeze, w_across, w_middle,
-            rise_mid, decode_mid, rise_fine, decode_fine, w_leave,
-        )
         constants = [jnp.asarray(m) for m in unpack_constants(z)]
-        operands = [owner, coefs, noisy, others, recv, bias, *constants, *weights]
+        w_pf = pool_fine.transpose(0, 2, 1).reshape(4 * n1, n2)
+        operands = [*constants, weights[0], w_pf, *weights[1:]]
         cells = z.cells
         return pl.pallas_call(
-            lambda *refs: net_kernel(z, *refs),
+            lambda *refs: net_kernel(z, len(operands), *refs),
             out_shape=(
                 jax.ShapeDtypeStruct(noisy.shape, BF),
                 jax.ShapeDtypeStruct(noisy.shape, F32),
             ),
-            in_specs=[smem, smem] + [vmem] * (len(operands) - 2),
+            in_specs=[smem] + [vmem] * 4 + [far] * len(operands),
             out_specs=(vmem, vmem),
-            scratch_shapes=[
+            scratch_shapes=[pltpu.VMEM(w.shape, BF) for w in operands]
+            + [
                 pltpu.VMEM((z.ext, cols + 128), BF),
                 pltpu.VMEM((z.gi * 40, 384), F32),
                 pltpu.VMEM((cells, 256), BF),
                 pltpu.VMEM((4, cells, 4 * n1), BF),
                 pltpu.VMEM((cells, 4 * n2), BF),
                 pltpu.VMEM((cells, n3), BF),
-                pltpu.VMEM((cells, z.slots * w_squeeze.shape[0]), BF),
+                pltpu.VMEM((cells, z.slots * inner), BF),
                 pltpu.VMEM((cells, 3 * n3), BF),
                 pltpu.VMEM((2, cells, 4 * n2), BF),
                 pltpu.VMEM((4, cells, 6 * n1), BF),
@@ -538,10 +652,11 @@
                 pltpu.VMEM((cells, 128), F32),
                 pltpu.VMEM((cells, 128), F32),
                 pltpu.VMEM((cells, 128), F32),
+                pltpu.SemaphoreType.DMA((len(operands),)),
             ],
-            compiler_params=pltpu.CompilerParams(vmem_limit_bytes=48 * 2**20),
+            compiler_params=pltpu.CompilerParams(vmem_limit_bytes=63 * 2**20),
             name="net",
-        )(*operands)
+        )(owner, noisy, others, recv, bias, *operands)
 
     copied = P()
     in_specs = (

time: 63.9 us -> 44.3 us (0.69); the launches traced: 62.7 us -> 44 us
  local copies, waits for them, and re-layouts: 28.2 us -> 1.4 us
  Pallas kernels: 21.7 us -> 28.2 us
  waiting for transfers between devices: 0.01 us -> 2.02 us
    unnamed x64 -> x8, local copies, waits for them, and re-layouts: 16.5 us -> 0.75 us
    pallas_call x1 -> x2, Pallas kernels: 19.7 us -> 26.1 us  [the longest x1 21.3 us: shards(): pl.pallas_call(lambda *refs: net_kernel(z, len(operands), *refs), out_sha...]
    reshape x5 -> x0, local copies, waits for them, and re-layouts: 4.78 us -> none  [the longest x1 1.82 us: lay_weights(): w_rm = rise_mid.transpose(2, 0, 1).reshape(n3, 4 * n2)]
    transpose x2 -> x0, local copies, waits for them, and re-layouts: 2.42 us -> none  [the longest x1 1.32 us: lay_weights(): w.reshape(6, 3, 2, 6, 16 * n1).transpose(2, 1, 3, 0, 4)]
    all_to_all x1, waiting for transfers between devices: 0.01 us -> 2.02 us  [shards(): recv = lax.all_to_all(send, AXES, 0, 0, tiled=True)]
    another operation x2 -> x0, local copies, waits for them, and re-layouts: 1.67 us -> none  [lay_weights(): w = jnp.stack(parts, axis=3)]
    pad x4 -> x0, local copies, waits for them, and re-layouts: 1.56 us -> none  [the longest x1 1.07 us: lay_weights(): w_lv = jnp.pad(w_lv, ((0, 0), (0, 0), (0, 128 - w_lv.shape[2])))]
  transfers between devices with their start and end apart: 2 -> 2, of which waited for: 0 -> 1; matrix products, arithmetic and copies ran while one was open for 27% -> 3% of each run, Pallas kernels for 0% -> 11%
where the time goes in v1:
time: 44.3 us; the launch traced here: 44 us
  Pallas kernels  28.2 us (64%)
  starting transfers between devices  9.15 us (21%)
  between operations  2.54 us (6%)
  waiting for transfers between devices  2.02 us (5%)
  local copies, waits for them, and re-layouts  1.4 us (3%)
  matrix products  0.65 us (1%)
    pallas_call x1, Pallas kernels, shards(): pl.pallas_call(lambda *refs: net_kernel(z, len(operands), *refs), out_sha...  21.3 us
    all_to_all x1, starting transfers between devices, shards(): recv = lax.all_to_all(send, AXES, 0, 0, tiled=True)  7.31 us
    pallas_call x1, Pallas kernels, shards(): pl.pallas_call(lambda *refs: lay_kernel(z, len(raw), *refs), out_shape=tu...  4.73 us
    pallas_call x1, Pallas kernels, shards(): pl.pallas_call(lambda *refs: pack_kernel(z, *refs), out_shape=jax.ShapeDt...  2.12 us
    all_to_all x1, waiting for transfers between devices, shards(): recv = lax.all_to_all(send, AXES, 0, 0, tiled=True)  2.02 us
    ppermute x1, starting transfers between devices, shards(): others = lax.ppermute(tile, 'plane', [(0, 1), (1, 0)])[None]  1.83 us
  transfers between devices with their start and end apart: 2, of which 1 were waited for; matrix products, arithmetic and copies ran while one was open for 3% of the time, Pallas kernels for 11%

profile of v1, /device:TPU:0, one launch (start us, length us, event | category | flops | bytes accessed | tf_op | source)
XLA Modules:
  0.0 44.0 jit_solution(13387746803840955025)
XLA Ops:
  0.6 0.0 copy-start
  0.6 2.1 %pack.1 = bf16[32,40,128]{2,1,0:T(8,128)(2,1)} custom-call(bf16[1,3,64,128]{3,2,1,0:T(8,128)(2,1)} %refs_1_.4, bf16[1,2,3,32,64]{4,3,2,1,0:T(8,128)(2,1)} %refs_1_.3), custom_call_target="tpu_custom_call" | custom-call | tf_op jit(solution)/shard_map/pack/pallas_call | solution.py:566
  2.8 7.3 %all-to-all-start = ((bf16[32,40,128]{2,1,0:T(8,128)(2,1)}), bf16[32,40,128]{2,1,0:T(8,128)(2,1)S(1)}, u32[]{:S(2)}, u32[]{:S(2)}) async-start(bf16[32,40,128]{2,1,0:T(8,128)(2,1)} %pack.1), calls=%async_computation | async-start | bytes 655360 | tf_op jit(solution)/shard_map/all_to_all | solution.py:580
  10.1 0.0 copy-start.2
  10.1 4.7 %lay.1 = (bf16[3,64,128]{2,1,0:T(8,128)(2,1)}, bf16[256,1024]{1,0:T(8,128)(2,1)}, bf16[512,256]{1,0:T(8,128)(2,1)}, bf16[256,128]{1,0:T(8,128)(2,1)}, bf16[256,2...) custom-call(bf16[1,3,64,128]{3,2,1,0:T(8,128)(2,1)} %refs_1_.4, ...), custom_call_target="tpu_custom_call" | custom-call | flops 1000000000 | bytes 10000000 | tf_op jit(solution)/shard_map/lay/pallas_call | solution.py:597
  14.8 1.8 %collective-permute-start = (bf16[3,64,128]{2,1,0:T(8,128)(2,1)}, bf16[3,64,128]{2,1,0:T(8,128)(2,1)S(1)}, u32[]{:S(2)}, u32[]{:S(2)}) collective-permute-start(bf16[3,64,128]{2,1,0:T(8,128)(2,1)} %get-tuple-element.13), channel_id=1, source_target_pairs={{0,16},{16,0},{1,17},{17,1},{2,18},{18,2},{3,19},{19,3},{4,20},{20... | collective-permute-start | bytes 147464 | tf_op jit(solution)/shard_map/ppermute | solution.py:619
  17.4 0.0 copy-done.2
  17.4 0.2 fusion
  17.6 0.0 copy-done
  17.6 0.5 %fusion.6 = f32[1,448]{1,0:T(1,128)S(1)} fusion(f32[256,1]{0,1:T(1,128)S(1)} %bitcast.23, f32[256,448]{0,1:T(8,128)S(1)} %copy-done), kind=kOutput, calls=%fused_computation.9 | convolution fusion | flops 1376256 | bytes 461568 | tf_op jit(solution)/shard_map/dot_general | solution.py:453
  19.1 0.7 %concatenate.7 = f32[452]{0:T(512)} concatenate(f32[448]{0:T(512)S(1)} %bitcast.21, f32[1]{0:T(128)} %bitcast.7, f32[1]{0:T(128)} %bitcast.8, f32[1]{0:T(128)S(6)} %sqrt.16, f32[1]{0:T(128)S(6)} %sqrt.17), dimensions={0} | concatenate | bytes 3616 | tf_op jit(solution)/shard_map/concatenate | solution.py:585
  19.8 0.0 collective-permute-done
  19.8 0.0 copy-start.3
  19.8 2.0 %all-to-all-done.refs_3_ = bf16[32,40,128]{2,1,0:T(8,128)(2,1)S(1)} async-done(((bf16[32,40,128]{2,1,0:T(8,128)(2,1)}), bf16[32,40,128]{2,1,0:T(8,128)(2,1)S(1)}, u32[]{:S(2)}, u32[]{:S(2)}) %all-to-all-start) | async-done | bytes 327712 | tf_op jit(solution)/shard_map/all_to_all | solution.py:580
  21.8 0.0 copy-start.1
  21.8 0.0 copy-done.3
  21.8 0.7 %copy-done.1 = bf16[32,40,128]{2,1,0:T(8,128)(2,1)} copy-done((bf16[32,40,128]{2,1,0:T(8,128)(2,1)}, bf16[32,40,128]{2,1,0:T(8,128)(2,1)S(1)}, u32[]{:S(2)}) %copy-start.1) | copy-done | bytes 327704
  22.5 21.3 %net.1 = (bf16[1,3,64,128]{3,2,1,0:T(8,128)(2,1)}, f32[1,3,64,128]{3,2,1,0:T(8,128)}) custom-call(s32[1]{0:T(128)S(6)} %copy.27.refs_0_, bf16[1,3,64,128]{3,2,1,0:T(8,128)(2,1)} %refs_1_.4, bf16[1,3,64,128]{3,2,1,0:T(8,128)(2,1)} %bitcast.19, bf16[32,40,128]{2,1,0:T(8,128)(2,1)} %copy-done.1, f32[1,452]{1,0:T(1,128)} %bitcast.20, ...), custom_call_target="tpu_custom_call" | custom-call | tf_op jit(solution)/shard_map/net/pallas_call | solution.py:630
  (2 shorter events, 0.1 us)
Async XLA Ops:
  0.6 17.0 %copy-start = (f32[256,448]{0,1:T(8,128)S(1)}, f32[256,448]{0,1:T(8,128)}, u32[]{:S(2)}) copy-start(f32[256,448]{0,1:T(8,128)} %param.29) | copy-start | bytes 1376260
  2.8 19.0 %all-to-all-start = ((bf16[32,40,128]{2,1,0:T(8,128)(2,1)}), bf16[32,40,128]{2,1,0:T(8,128)(2,1)S(1)}, u32[]{:S(2)}, u32[]{:S(2)}) async-start(bf16[32,40,128]{2,1,0:T(8,128)(2,1)} %pack.1), calls=%async_computation | async-start | bytes 655360 | tf_op jit(solution)/shard_map/all_to_all | solution.py:580
  10.1 7.3 %copy-start.2 = (f32[64,256]{1,0:T(8,128)S(1)}, f32[64,256]{1,0:T(8,128)}, u32[]{:S(2)}) copy-start(f32[64,256]{1,0:T(8,128)} %param.28) | copy-start | bytes 196612
  14.8 4.9 %collective-permute-start = (bf16[3,64,128]{2,1,0:T(8,128)(2,1)}, bf16[3,64,128]{2,1,0:T(8,128)(2,1)S(1)}, u32[]{:S(2)}, u32[]{:S(2)}) collective-permute-start(bf16[3,64,128]{2,1,0:T(8,128)(2,1)} %get-tuple-element.13), channel_id=1, source_target_pairs={{0,16},{16,0},{1,17},{17,1},{2,18},{18,2},{3,19},{19,3},{4,20},{20... | collective-permute-start | bytes 147464 | tf_op jit(solution)/shard_map/ppermute | solution.py:619
  19.8 2.0 %copy-start.3 = (bf16[3,64,128]{2,1,0:T(8,128)(2,1)}, bf16[3,64,128]{2,1,0:T(8,128)(2,1)S(1)}, u32[]{:S(2)}) copy-start(bf16[3,64,128]{2,1,0:T(8,128)(2,1)S(1)} %collective-permute-done) | copy-start | bytes 147460
  21.8 0.7 %copy-start.1 = (bf16[32,40,128]{2,1,0:T(8,128)(2,1)}, bf16[32,40,128]{2,1,0:T(8,128)(2,1)S(1)}, u32[]{:S(2)}) copy-start(bf16[32,40,128]{2,1,0:T(8,128)(2,1)S(1)} %all-to-all-done.refs_3_) | copy-start | bytes 983044

commit v2 on v1

--- a/solution.py
+++ b/solution.py
@@ -108,7 +108,7 @@
                 for o in range(3):
                     gather[b, o * z.rows + 4 * i + a, i * 24 + a * 6 + b * 3 + o] = 1
     return tuple(
-        m.astype(BF) for m in (across, lift.reshape(-1, 6 * 64), down, sides, spread, gather)
+        m.astype(BF) for m in (sides, across, lift.reshape(-1, 6 * 64), down, spread, gather)
     )
 
 
@@ -221,15 +221,16 @@
 
 
 def net_kernel(
-    z, count, owner, noisy, others, recv, bias, *refs
+    z, count, owner, recv, others, *refs
 ):
     far, refs = refs[:count], refs[count:]
-    pred, sample, refs = refs[0], refs[1], refs[2:]
+    pred_far, sample_far, refs = refs[0], refs[1], refs[2:]
     near, refs = refs[:count], refs[count:]
-    ext, grid, entry, h1, d1, d2, sq, mx, v2, v1, e1, last, mask, half, halfp, sems = refs
+    (pred, sample, ext, grid, entry, h1, d1, d2, sq, mx, v2, v1, e1, last,
+     mask, half, halfp, sems, out_sems) = refs
     copies = fetch(tuple(zip(far, near)), sems)
-    across, lift, down, sides, spread, gather = near[:6]
-    w_in, w_pf, w_pm, w_sq, w_ac, w_mid, w_rm, w_dm, w_rf, w_df, w_lv = near[6:]
+    noisy, sides, across, lift, down, bias = near[:6]
+    w_in, w_pf, w_pm, w_sq, w_ac, w_mid, w_rm, w_dm, w_rf, w_df, w_lv, spread, gather = near[6:]
     plane, span, height = (lax.axis_index(a) for a in AXES)
     step, gi = z.step, z.gi
     n1, n2, n3 = w_in.shape[1] // 16, w_pf.shape[1], w_pm.shape[1]
@@ -253,12 +254,7 @@
         return x * jnp.concatenate([m] * (x.shape[1] // 128), axis=1)
 
     lanes = lax.broadcasted_iota(jnp.int32, (z.strip, 128), 1)
-    b1 = bias[:, 0:n1]
-    b1 = jnp.concatenate([b1] * 4, axis=1)
-    b2 = bias[:, n1 : n1 + n2]
-    b3 = bias[:, n1 + n2 : n1 + n2 + n3]
-
-    for copy in copies[:4]:
+    for copy in copies[:5]:
         copy.wait()
     for k in range(z.slots):
         q = z.planes_of(plane)[k]
@@ -309,9 +305,13 @@
             entry[at : at + step, 0:128] = turned[0:step].astype(BF)
             entry[at : at + step, 128:256] = turned[64 : 64 + step].astype(BF)
         if k == 0:
-            for copy in copies[6:10]:
+            for copy in copies[5:10]:
                 copy.wait()
-        per = 5 if gi % 5 == 0 else 1
+            b1 = bias[:, 0:n1]
+            b1 = jnp.concatenate([b1] * 4, axis=1)
+            b2 = bias[:, n1 : n1 + n2]
+            b3 = bias[:, n1 + n2 : n1 + n2 + n3]
+        per = gi
         for i in range(0, gi, per):
             rows = slice(i * step, (i + per) * step)
             x = entry[rows, :]
@@ -341,7 +341,7 @@
     def span_of(i, n, shift=0):
         return slice((i + shift) * step, (i + shift + n) * step)
 
-    for copy in copies[4:6] + copies[10:]:
+    for copy in copies[10:]:
         copy.wait()
     for i, n in chunks(0, gi, 5):
         rows = span_of(i, n)
@@ -351,13 +351,10 @@
         mx[rows, 0:n3] = pltpu.roll(m, 1, 0).astype(BF)
         mx[rows, 2 * n3 : 3 * n3] = pltpu.roll(m, n * step - 1, 0).astype(BF)
 
-    for i, n in chunks(1, gi - 1, 6):
+    for i, n in chunks(1, gi - 1, 18):
         rows = span_of(i, n)
-        c = None
-        for a in range(3):
-            part = dot(mx[span_of(i, n, a - 1), :], w_mid[a])
-            c = part if c is None else c + part
-        c = silu(c).astype(BF)
+        wide = [mx[span_of(i, n, a - 1), :] for a in range(3)]
+        c = silu(dot(jnp.concatenate(wide, axis=1), w_mid[...])).astype(BF)
         v = dot(c, w_rm[...]) + d1[rows, :].astype(F32)
         v = masked(v, rows)
         for p in range(2):
@@ -367,14 +364,12 @@
             v2[p, rows, 3 * n2 : 4 * n2] = pltpu.roll(vp[:, :n2], n * step - 1, 0).astype(BF)
 
     for p in range(2):
-        for i, n in chunks(2 - p, gi - 1 - p, 6):
+        for i, n in chunks(2 - p, gi - 1 - p, 17):
             rows = span_of(i, n)
-            e = None
-            for a in range(3):
-                at = p + a - 1
-                part = dot(v2[at % 2, span_of(i, n, at // 2), :], w_dm[a])
-                e = part if e is None else e + part
-            e = silu(e).astype(BF)
+            wide = [
+                v2[at % 2, span_of(i, n, at // 2), :] for at in range(p - 1, p + 2)
+            ]
+            e = silu(dot(jnp.concatenate(wide, axis=1), w_dm[...])).astype(BF)
             for q in range(2):
                 v = dot(e[:, q * n2 : (q + 1) * n2], w_rf[...])
                 v = masked(v + h1[2 * p + q, rows, :].astype(F32), rows)
@@ -390,14 +385,12 @@
         for i, n in chunks(2 - turn, gi - 2, 6):
             rows = span_of(i, n)
             for pair in range(2):
-                x = None
-                for a in range(4):
-                    at = 2 * turn + a
-                    part = dot(
-                        v1[at % 4, span_of(i, n, at // 4), 2 * pair * n1 : (2 * pair + 4) * n1],
-                        w_df[a],
-                    )
-                    x = part if x is None else x + part
+                lanes_in = slice(2 * pair * n1, (2 * pair + 4) * n1)
+                wide = [
+                    v1[at % 4, span_of(i, n, at // 4), lanes_in]
+                    for at in range(2 * turn, 2 * turn + 4)
+                ]
+                x = dot(jnp.concatenate(wide, axis=1), w_df[...])
                 for a in range(2):
                     at = 2 * turn + 1 + a
                     there = span_of(i, n, at // 4)
@@ -414,15 +407,9 @@
     for i, n in chunks(2, gi - 2, 8):
         outs = []
         for pair in range(2):
-            x = None
-            for a in range(6):
-                at = a - 1
-                part = dot(
-                    e1[at % 4, span_of(i, n, at // 4), 2 * pair * n1 : (2 * pair + 4) * n1],
-                    w_lv[a],
-                )
-                x = part if x is None else x + part
-            outs.append(x)
+            lanes_in = slice(2 * pair * n1, (2 * pair + 4) * n1)
+            wide = [e1[at % 4, span_of(i, n, at // 4), lanes_in] for at in range(-1, 5)]
+            outs.append(dot(jnp.concatenate(wide, axis=1), w_lv[...]))
         for r in range(n):
             block = jnp.concatenate([o[r * step : (r + 1) * step] for o in outs], axis=0)
             turned = jnp.transpose(block)[0:24]
@@ -432,11 +419,17 @@
     guess = dot(gather[0], spread_out[:, 0 : z.cols])
     guess = guess + dot(gather[1], spread_out[:, z.cols :])
     pred[0] = guess.astype(BF).reshape(3, z.rows, z.cols)
+    pred_copy = pltpu.make_async_copy(pred, pred_far, out_sems.at[0])
+    pred_copy.start()
     given = noisy[0].reshape(3 * z.rows, z.cols).astype(F32)
     at = n1 + n2 + n3
     back, rise, keep, add = (bias[:, at + t : at + t + 1] for t in range(4))
     result = keep * ((given - back * guess) * rise) + add * guess
     sample[0] = result.reshape(3, z.rows, z.cols)
+    sample_copy = pltpu.make_async_copy(sample, sample_far, out_sems.at[1])
+    sample_copy.start()
+    pred_copy.wait()
+    sample_copy.wait()
 
 
 def plan(stepnum):
@@ -509,7 +502,7 @@
                     pick = jnp.where(hit, 1.0, pick)
             part = dot(tall[b], pick.astype(BF))
             total = part if total is None else total + part
-        w_lv[y] = total.astype(BF)
+        w_lv[y * 4 * n1 : (y + 1) * 4 * n1, :] = total.astype(BF)
 
     for y in range(4):
         for pair in range(2):
@@ -530,11 +523,12 @@
     for k, tap in enumerate(taps):
         w_ac[k * width : (k + 1) * width, :] = jnp.transpose(tap)
     for a in range(3):
-        w_mid[a] = jnp.transpose(w_middle[a])
+        w_mid[a * 3 * n3 : (a + 1) * 3 * n3, :] = jnp.transpose(w_middle[a])
         turned = jnp.transpose(decode_mid[a])
-        w_dm[a] = jnp.zeros((4 * n2, 2 * n2), BF)
-        w_dm[a, 0 : 3 * n2, 0:n2] = turned
-        w_dm[a, n2 : 4 * n2, n2 : 2 * n2] = turned
+        at = a * 4 * n2
+        w_dm[at : at + 4 * n2, :] = jnp.zeros((4 * n2, 2 * n2), BF)
+        w_dm[at : at + 3 * n2, 0:n2] = turned
+        w_dm[at + n2 : at + 4 * n2, n2 : 2 * n2] = turned
     w_rf[...] = jnp.transpose(rise_fine[...].reshape(4 * n1, n2))
 
     nat[...] = jnp.zeros_like(nat)
@@ -547,7 +541,7 @@
             for r in range(2):
                 nat[a + r, (2 * r + b) * n1 : (2 * r + b + 1) * n1, :] = wide.astype(BF)
     for a in range(4):
-        w_df[a] = jnp.transpose(nat[a])
+        w_df[a * 4 * n1 : (a + 1) * 4 * n1, :] = jnp.transpose(nat[a])
 
 
 def solution(mesh):
@@ -591,8 +585,8 @@
         shapes = (
             noisy.shape[1:],
             (256, 16 * n1), (4 * n2, n3), (n3, inner), (z.slots * inner, n3),
-            (3, 3 * n3, n3), (n3, 4 * n2), (3, 4 * n2, 2 * n2), (n2, 4 * n1),
-            (4, 4 * n1, 4 * n1), (6, 4 * n1, 128),
+            (9 * n3, n3), (n3, 4 * n2), (12 * n2, 2 * n2), (n2, 4 * n1),
+            (16 * n1, 4 * n1), (24 * n1, 128),
         )
         tile, *weights = pl.pallas_call(
             lambda *refs: lay_kernel(z, len(raw), *refs),
@@ -625,7 +619,10 @@
             )
         constants = [jnp.asarray(m) for m in unpack_constants(z)]
         w_pf = pool_fine.transpose(0, 2, 1).reshape(4 * n1, n2)
-        operands = [*constants, weights[0], w_pf, *weights[1:]]
+        operands = [
+            noisy, *constants[:4], bias, weights[0], w_pf, *weights[1:],
+            *constants[4:],
+        ]
         cells = z.cells
         return pl.pallas_call(
             lambda *refs: net_kernel(z, len(operands), *refs),
@@ -633,10 +630,12 @@
                 jax.ShapeDtypeStruct(noisy.shape, BF),
                 jax.ShapeDtypeStruct(noisy.shape, F32),
             ),
-            in_specs=[smem] + [vmem] * 4 + [far] * len(operands),
-            out_specs=(vmem, vmem),
-            scratch_shapes=[pltpu.VMEM(w.shape, BF) for w in operands]
+            in_specs=[smem, vmem, vmem] + [far] * len(operands),
+            out_specs=(far, far),
+            scratch_shapes=[pltpu.VMEM(w.shape, w.dtype) for w in operands]
             + [
+                pltpu.VMEM(noisy.shape, BF),
+                pltpu.VMEM(noisy.shape, F32),
                 pltpu.VMEM((z.ext, cols + 128), BF),
                 pltpu.VMEM((z.gi * 40, 384), F32),
                 pltpu.VMEM((cells, 256), BF),
@@ -653,10 +652,11 @@
                 pltpu.VMEM((cells, 128), F32),
                 pltpu.VMEM((cells, 128), F32),
                 pltpu.SemaphoreType.DMA((len(operands),)),
+                pltpu.SemaphoreType.DMA((2,)),
             ],
             compiler_params=pltpu.CompilerParams(vmem_limit_bytes=63 * 2**20),
             name="net",
-        )(owner, noisy, others, recv, bias, *operands)
+        )(owner, recv, others, *operands)
 
     copied = P()
     in_specs = (

time: 44.3 us -> 41.1 us (0.928)
  Pallas kernels: 28.2 us -> 25.2 us
    pallas_call x1, Pallas kernels: 21.3 us -> 18.4 us  [shards(): pl.pallas_call(lambda *refs: net_kernel(z, len(operands), *refs), out_sha...]
  transfers between devices with their start and end apart: 2 -> 2, of which waited for: 1 -> 1; matrix products, arithmetic and copies ran while one was open for 3% -> 3% of each run, Pallas kernels for 11% -> 12%
where the time goes in v2:
time: 41.1 us; the launch traced here: 40.9 us
  Pallas kernels  25.2 us (61%)
  starting transfers between devices  9.15 us (22%)
  between operations  2.38 us (6%)
  waiting for transfers between devices  2.02 us (5%)
  local copies, waits for them, and re-layouts  1.4 us (3%)
  matrix products  0.65 us (2%)
    pallas_call x1, Pallas kernels, shards(): pl.pallas_call(lambda *refs: net_kernel(z, len(operands), *refs), out_sha...  18.4 us
    all_to_all x1, starting transfers between devices, shards(): recv = lax.all_to_all(send, AXES, 0, 0, tiled=True)  7.31 us
    pallas_call x1, Pallas kernels, shards(): pl.pallas_call(lambda *refs: lay_kernel(z, len(raw), *refs), out_shape=tu...  4.74 us
    pallas_call x1, Pallas kernels, shards(): pl.pallas_call(lambda *refs: pack_kernel(z, *refs), out_shape=jax.ShapeDt...  2.12 us
    all_to_all x1, waiting for transfers between devices, shards(): recv = lax.all_to_all(send, AXES, 0, 0, tiled=True)  2.02 us
    ppermute x1, starting transfers between devices, shards(): others = lax.ppermute(tile, 'plane', [(0, 1), (1, 0)])[None]  1.83 us
  transfers between devices with their start and end apart: 2, of which 1 were waited for; matrix products, arithmetic and copies ran while one was open for 3% of the time, Pallas kernels for 12%

profile of v2, /device:TPU:0, one launch (start us, length us, event | category | flops | bytes accessed | tf_op | source)
XLA Modules:
  0.0 40.9 jit_solution(1089656394887790883)
XLA Ops:
  0.6 0.0 copy-start
  0.6 2.1 %pack.1 = bf16[32,40,128]{2,1,0:T(8,128)(2,1)} custom-call(bf16[1,3,64,128]{3,2,1,0:T(8,128)(2,1)} %refs_3_.3, bf16[1,2,3,32,64]{4,3,2,1,0:T(8,128)(2,1)} %refs_1_.2), custom_call_target="tpu_custom_call" | custom-call | tf_op jit(solution)/shard_map/pack/pallas_call | solution.py:560
  2.8 7.3 %all-to-all-start = ((bf16[32,40,128]{2,1,0:T(8,128)(2,1)}), bf16[32,40,128]{2,1,0:T(8,128)(2,1)S(1)}, u32[]{:S(2)}, u32[]{:S(2)}) async-start(bf16[32,40,128]{2,1,0:T(8,128)(2,1)} %pack.1), calls=%async_computation | async-start | bytes 655360 | tf_op jit(solution)/shard_map/all_to_all | solution.py:574
  10.1 0.0 copy-start.2
  10.1 4.7 %lay.1 = (bf16[3,64,128]{2,1,0:T(8,128)(2,1)}, bf16[256,1024]{1,0:T(8,128)(2,1)}, bf16[512,256]{1,0:T(8,128)(2,1)}, bf16[256,128]{1,0:T(8,128)(2,1)}, bf16[256,2...) custom-call(bf16[1,3,64,128]{3,2,1,0:T(8,128)(2,1)} %refs_3_.3, ...), custom_call_target="tpu_custom_call" | custom-call | flops 1000000000 | bytes 10000000 | tf_op jit(solution)/shard_map/lay/pallas_call | solution.py:591
  14.9 1.8 %collective-permute-start = (bf16[3,64,128]{2,1,0:T(8,128)(2,1)}, bf16[3,64,128]{2,1,0:T(8,128)(2,1)S(1)}, u32[]{:S(2)}, u32[]{:S(2)}) collective-permute-start(bf16[3,64,128]{2,1,0:T(8,128)(2,1)} %get-tuple-element.13), channel_id=1, source_target_pairs={{0,16},{16,0},{1,17},{17,1},{2,18},{18,2},{3,19},{19,3},{4,20},{20... | collective-permute-start | bytes 147464 | tf_op jit(solution)/shard_map/ppermute | solution.py:613
  17.4 0.0 copy-done.2
  17.4 0.2 fusion
  17.6 0.0 copy-done
  17.6 0.5 %fusion.6 = f32[1,448]{1,0:T(1,128)S(1)} fusion(f32[256,1]{0,1:T(1,128)S(1)} %bitcast.23, f32[256,448]{0,1:T(8,128)S(1)} %copy-done), kind=kOutput, calls=%fused_computation.9 | convolution fusion | flops 1376256 | bytes 461568 | tf_op jit(solution)/shard_map/dot_general | solution.py:446
  19.1 0.7 %concatenate.7 = f32[452]{0:T(512)} concatenate(f32[448]{0:T(512)S(1)} %bitcast.21, f32[1]{0:T(128)} %bitcast.7, f32[1]{0:T(128)} %bitcast.8, f32[1]{0:T(128)S(6)} %sqrt.16, f32[1]{0:T(128)S(6)} %sqrt.17), dimensions={0} | concatenate | bytes 3616 | tf_op jit(solution)/shard_map/concatenate | solution.py:579
  19.8 0.0 collective-permute-done
  19.8 0.0 copy-start.3
  19.8 2.0 %all-to-all-done.refs_1_ = bf16[32,40,128]{2,1,0:T(8,128)(2,1)S(1)} async-done(((bf16[32,40,128]{2,1,0:T(8,128)(2,1)}), bf16[32,40,128]{2,1,0:T(8,128)(2,1)S(1)}, u32[]{:S(2)}, u32[]{:S(2)}) %all-to-all-start) | async-done | bytes 327712 | tf_op jit(solution)/shard_map/all_to_all | solution.py:574
  21.8 0.0 copy-start.1
  21.8 0.0 copy-done.3
  21.8 0.7 %copy-done.1 = bf16[32,40,128]{2,1,0:T(8,128)(2,1)} copy-done((bf16[32,40,128]{2,1,0:T(8,128)(2,1)}, bf16[32,40,128]{2,1,0:T(8,128)(2,1)S(1)}, u32[]{:S(2)}) %copy-start.1) | copy-done | bytes 327704
  22.5 18.4 %net.1 = (bf16[1,3,64,128]{3,2,1,0:T(8,128)(2,1)}, f32[1,3,64,128]{3,2,1,0:T(8,128)}) custom-call(s32[1]{0:T(128)S(6)} %copy.27.refs_0_, bf16[32,40,128]{2,1,0:T(8,128)(2,1)} %copy-done.1, bf16[1,3,64,128]{3,2,1,0:T(8,128)(2,1)} %bitcast.19, bf16[1,3,64,128]{3,2,1,0:T(8,128)(2,1)} %refs_3_.3, bf16[32,128]{1,0:T(8,128)(2,1)} %constant.45.clone.refs_4_, ...), custom_call_target="tpu_custom_call" | custom-call | tf_op jit(solution)/shard_map/net/pallas_call | solution.py:627
  (2 shorter events, 0.1 us)
Async XLA Ops:
  0.6 17.0 %copy-start = (f32[256,448]{0,1:T(8,128)S(1)}, f32[256,448]{0,1:T(8,128)}, u32[]{:S(2)}) copy-start(f32[256,448]{0,1:T(8,128)} %param.29) | copy-start | bytes 1376260
  2.8 19.0 %all-to-all-start = ((bf16[32,40,128]{2,1,0:T(8,128)(2,1)}), bf16[32,40,128]{2,1,0:T(8,128)(2,1)S(1)}, u32[]{:S(2)}, u32[]{:S(2)}) async-start(bf16[32,40,128]{2,1,0:T(8,128)(2,1)} %pack.1), calls=%async_computation | async-start | bytes 655360 | tf_op jit(solution)/shard_map/all_to_all | solution.py:574
  10.1 7.3 %copy-start.2 = (f32[64,256]{1,0:T(8,128)S(1)}, f32[64,256]{1,0:T(8,128)}, u32[]{:S(2)}) copy-start(f32[64,256]{1,0:T(8,128)} %param.28) | copy-start | bytes 196612
  14.9 4.9 %collective-permute-start = (bf16[3,64,128]{2,1,0:T(8,128)(2,1)}, bf16[3,64,128]{2,1,0:T(8,128)(2,1)S(1)}, u32[]{:S(2)}, u32[]{:S(2)}) collective-permute-start(bf16[3,64,128]{2,1,0:T(8,128)(2,1)} %get-tuple-element.13), channel_id=1, source_target_pairs={{0,16},{16,0},{1,17},{17,1},{2,18},{18,2},{3,19},{19,3},{4,20},{20... | collective-permute-start | bytes 147464 | tf_op jit(solution)/shard_map/ppermute | solution.py:613
  19.8 2.0 %copy-start.3 = (bf16[3,64,128]{2,1,0:T(8,128)(2,1)}, bf16[3,64,128]{2,1,0:T(8,128)(2,1)S(1)}, u32[]{:S(2)}) copy-start(bf16[3,64,128]{2,1,0:T(8,128)(2,1)S(1)} %collective-permute-done) | copy-start | bytes 147460
  21.8 0.7 %copy-start.1 = (bf16[32,40,128]{2,1,0:T(8,128)(2,1)}, bf16[32,40,128]{2,1,0:T(8,128)(2,1)S(1)}, u32[]{:S(2)}) copy-start(bf16[32,40,128]{2,1,0:T(8,128)(2,1)S(1)} %all-to-all-done.refs_1_) | copy-start | bytes 983044

commit v3 on v2

--- a/solution.py
+++ b/solution.py
@@ -42,7 +42,7 @@
         self.cond_rows, self.cond_cols = cond_rows, cond_cols
         self.devices = planes * spans * heights
         self.gi, self.gj = rows // 4 + 2 * EDGE, cols // 4 + 2 * EDGE
-        self.step = up(self.gj, 16)
+        self.step = up(self.gj, 8)
         self.cells = self.gi * self.step
         self.slots = min(planes, 3)
         self.strip = up(3 * RIM, 16)
@@ -221,7 +221,7 @@
 
 
 def net_kernel(
-    z, count, owner, recv, others, *refs
+    z, count, owner, *refs
 ):
     far, refs = refs[:count], refs[count:]
     pred_far, sample_far, refs = refs[0], refs[1], refs[2:]
@@ -229,8 +229,8 @@
     (pred, sample, ext, grid, entry, h1, d1, d2, sq, mx, v2, v1, e1, last,
      mask, half, halfp, sems, out_sems) = refs
     copies = fetch(tuple(zip(far, near)), sems)
-    noisy, sides, across, lift, down, bias = near[:6]
-    w_in, w_pf, w_pm, w_sq, w_ac, w_mid, w_rm, w_dm, w_rf, w_df, w_lv, spread, gather = near[6:]
+    recv, others, noisy, sides, across, lift, down, bias = near[:8]
+    w_in, w_pf, w_pm, w_sq, w_ac, w_mid, w_rm, w_dm, w_rf, w_df, w_lv, spread, gather = near[8:]
     plane, span, height = (lax.axis_index(a) for a in AXES)
     step, gi = z.step, z.gi
     n1, n2, n3 = w_in.shape[1] // 16, w_pf.shape[1], w_pm.shape[1]
@@ -254,7 +254,7 @@
         return x * jnp.concatenate([m] * (x.shape[1] // 128), axis=1)
 
     lanes = lax.broadcasted_iota(jnp.int32, (z.strip, 128), 1)
-    for copy in copies[:5]:
+    for copy in copies[:7]:
         copy.wait()
     for k in range(z.slots):
         q = z.planes_of(plane)[k]
@@ -302,10 +302,10 @@
             )
             turned = jnp.transpose(stack)
             at = i * step
-            entry[at : at + step, 0:128] = turned[0:step].astype(BF)
-            entry[at : at + step, 128:256] = turned[64 : 64 + step].astype(BF)
+            entry[at : at + step, 0:128] = turned[0:step]
+            entry[at : at + step, 128:256] = turned[64 : 64 + step]
         if k == 0:
-            for copy in copies[5:10]:
+            for copy in copies[7:12]:
                 copy.wait()
             b1 = bias[:, 0:n1]
             b1 = jnp.concatenate([b1] * 4, axis=1)
@@ -314,7 +314,7 @@
         per = gi
         for i in range(0, gi, per):
             rows = slice(i * step, (i + per) * step)
-            x = entry[rows, :]
+            x = entry[rows, :].astype(BF)
             mids = []
             for g in range(4):
                 h = dot(x, w_in[:, g * 4 * n1 : (g + 1) * 4 * n1]) + b1
@@ -331,90 +331,91 @@
             width = w_sq.shape[1]
             sq[rows, k * width : (k + 1) * width] = dot(low, w_sq[...]).astype(BF)
 
-    def chunks(first, last_, per):
-        out = []
-        while first < last_:
-            out.append((first, min(per, last_ - first)))
-            first += per
-        return out
-
-    def span_of(i, n, shift=0):
-        return slice((i + shift) * step, (i + shift + n) * step)
-
-    for copy in copies[10:]:
+    def rows_of(first, last_):
+        return slice(first * step // 16 * 16, up(last_ * step, 16))
+
+    def above(x):
+        return jnp.concatenate([x[-step:], x[:-step]], axis=0)
+
+    def below(x):
+        return jnp.concatenate([x[step:], x[:step]], axis=0)
+
+    for copy in copies[12:]:
         copy.wait()
-    for i, n in chunks(0, gi, 5):
-        rows = span_of(i, n)
-        m = d2[rows, :].astype(F32) + dot(sq[rows, :], w_ac[...])
-        m = masked(m, rows)
-        mx[rows, n3 : 2 * n3] = m.astype(BF)
-        mx[rows, 0:n3] = pltpu.roll(m, 1, 0).astype(BF)
-        mx[rows, 2 * n3 : 3 * n3] = pltpu.roll(m, n * step - 1, 0).astype(BF)
-
-    for i, n in chunks(1, gi - 1, 18):
-        rows = span_of(i, n)
-        wide = [mx[span_of(i, n, a - 1), :] for a in range(3)]
-        c = silu(dot(jnp.concatenate(wide, axis=1), w_mid[...])).astype(BF)
-        v = dot(c, w_rm[...]) + d1[rows, :].astype(F32)
-        v = masked(v, rows)
-        for p in range(2):
-            vp = v[:, 2 * p * n2 : 2 * (p + 1) * n2]
-            v2[p, rows, n2 : 3 * n2] = vp.astype(BF)
-            v2[p, rows, 0:n2] = pltpu.roll(vp[:, n2:], 1, 0).astype(BF)
-            v2[p, rows, 3 * n2 : 4 * n2] = pltpu.roll(vp[:, :n2], n * step - 1, 0).astype(BF)
-
+    m = d2[...].astype(F32) + dot(sq[...], w_ac[...])
+    m = masked(m, slice(0, z.cells))
+    for a, ma in enumerate((above(m), m, below(m))):
+        at = 3 * n3 * a
+        mx[:, at + n3 : at + 2 * n3] = ma.astype(BF)
+    for b, mb in enumerate((pltpu.roll(m, 1, 0), pltpu.roll(m, z.cells - 1, 0))):
+        for a, ma in enumerate((above(mb), mb, below(mb))):
+            at = 3 * n3 * a + 2 * b * n3
+            mx[:, at : at + n3] = ma.astype(BF)
+
+    rows = rows_of(1, gi - 1)
+    n = rows.stop - rows.start
+    c = silu(dot(mx[rows, :], w_mid[...])).astype(BF)
+    v = dot(c, w_rm[...]) + d1[rows, :].astype(F32)
+    v = masked(v, rows)
     for p in range(2):
-        for i, n in chunks(2 - p, gi - 1 - p, 17):
-            rows = span_of(i, n)
-            wide = [
-                v2[at % 2, span_of(i, n, at // 2), :] for at in range(p - 1, p + 2)
-            ]
-            e = silu(dot(jnp.concatenate(wide, axis=1), w_dm[...])).astype(BF)
-            for q in range(2):
-                v = dot(e[:, q * n2 : (q + 1) * n2], w_rf[...])
-                v = masked(v + h1[2 * p + q, rows, :].astype(F32), rows)
-                for a in range(2):
-                    va = v[:, 2 * a * n1 : 2 * (a + 1) * n1]
-                    v1[2 * p + a, rows, 2 * q * n1 : 2 * (q + 1) * n1] = va.astype(BF)
-                    if q == 0:
-                        v1[2 * p + a, rows, 4 * n1 : 6 * n1] = pltpu.roll(
-                            va, n * step - 1, 0
-                        ).astype(BF)
+        vp = v[:, 2 * p * n2 : 2 * (p + 1) * n2]
+        left = pltpu.roll(vp[:, n2:], 1, 0)
+        right = pltpu.roll(vp[:, :n2], n - 1, 0)
+        turn = below if p == 0 else above
+        for at, part in ((n2, vp), (0, left), (3 * n2, right)):
+            v2[p, rows, at : at + part.shape[1]] = part.astype(BF)
+            v2[3 - p, rows, at : at + part.shape[1]] = turn(part).astype(BF)
+
+    for p in range(2):
+        rows = rows_of(1, gi - 1 - p)
+        n = rows.stop - rows.start
+        wide = [v2[at, rows, :] for at in ((2, 0, 1), (0, 1, 3))[p]]
+        e = silu(dot(jnp.concatenate(wide, axis=1), w_dm[...])).astype(BF)
+        for q in range(2):
+            v = dot(e[:, q * n2 : (q + 1) * n2], w_rf[...])
+            v = masked(v + h1[2 * p + q, rows, :].astype(F32), rows)
+            for a in range(2):
+                va = v[:, 2 * a * n1 : 2 * (a + 1) * n1]
+                parts = [(2 * q * n1, va)]
+                if q == 0:
+                    parts.append((4 * n1, pltpu.roll(va, n - 1, 0)))
+                for at, part in parts:
+                    v1[2 * p + a, rows, at : at + 2 * n1] = part.astype(BF)
+                    if p == 0:
+                        v1[4 + a, rows, at : at + 2 * n1] = below(part).astype(BF)
 
     for turn in range(2):
-        for i, n in chunks(2 - turn, gi - 2, 6):
-            rows = span_of(i, n)
-            for pair in range(2):
-                lanes_in = slice(2 * pair * n1, (2 * pair + 4) * n1)
-                wide = [
-                    v1[at % 4, span_of(i, n, at // 4), lanes_in]
-                    for at in range(2 * turn, 2 * turn + 4)
-                ]
-                x = dot(jnp.concatenate(wide, axis=1), w_df[...])
-                for a in range(2):
-                    at = 2 * turn + 1 + a
-                    there = span_of(i, n, at // 4)
-                    t = masked(
-                        x[:, 2 * a * n1 : 2 * (a + 1) * n1], there, halfp if pair else half
-                    )
-                    t = t + t * jnp.tanh(t)
-                    if pair == 0:
-                        e1[at % 4, there, 2 * n1 : 4 * n1] = t.astype(BF)
-                    else:
-                        e1[at % 4, there, 4 * n1 : 6 * n1] = t.astype(BF)
-                        e1[at % 4, there, 0 : 2 * n1] = pltpu.roll(t, 1, 0).astype(BF)
-
-    for i, n in chunks(2, gi - 2, 8):
-        outs = []
+        rows = rows_of(2 - turn, gi - 2)
+        n = rows.stop - rows.start
         for pair in range(2):
             lanes_in = slice(2 * pair * n1, (2 * pair + 4) * n1)
-            wide = [e1[at % 4, span_of(i, n, at // 4), lanes_in] for at in range(-1, 5)]
-            outs.append(dot(jnp.concatenate(wide, axis=1), w_lv[...]))
-        for r in range(n):
-            block = jnp.concatenate([o[r * step : (r + 1) * step] for o in outs], axis=0)
-            turned = jnp.transpose(block)[0:24]
-            at = (i - 2 + r) * 24
-            last[at : at + 24, :] = turned
+            wide = [v1[at, rows, lanes_in] for at in ((0, 1, 2, 3), (2, 3, 4, 5))[turn]]
+            x = dot(jnp.concatenate(wide, axis=1), w_df[...])
+            for a in range(2):
+                shift = step if turn and a else 0
+                there = slice(rows.start + shift, rows.stop + shift)
+                t = masked(
+                    x[:, 2 * a * n1 : 2 * (a + 1) * n1], there, halfp if pair else half
+                )
+                t = t + t * jnp.tanh(t)
+                parts = [((2 + 2 * pair) * n1, t)]
+                if pair == 1:
+                    parts.append((0, pltpu.roll(t, 1, 0)))
+                for at, part in parts:
+                    e1[2 * turn + a, rows, at : at + 2 * n1] = part.astype(BF)
+                    if turn:
+                        e1[4 + a, rows, at : at + 2 * n1] = above(part).astype(BF)
+
+    rows = rows_of(2, gi - 2)
+    outs = []
+    for pair in range(2):
+        lanes_in = slice(2 * pair * n1, (2 * pair + 4) * n1)
+        wide = [e1[at, rows, lanes_in] for at in (4, 5, 0, 1, 2, 3)]
+        outs.append(dot(jnp.concatenate(wide, axis=1), w_lv[...]))
+    for r in range(inner):
+        at = (2 + r) * step - rows.start
+        block = jnp.concatenate([o[at : at + step] for o in outs], axis=0)
+        last[r * 24 : (r + 1) * 24, :] = jnp.transpose(block)[0:24]
     spread_out = dot(last[...].astype(BF), spread[...]).astype(BF)
     guess = dot(gather[0], spread_out[:, 0 : z.cols])
     guess = guess + dot(gather[1], spread_out[:, z.cols :])
@@ -620,7 +621,7 @@
         constants = [jnp.asarray(m) for m in unpack_constants(z)]
         w_pf = pool_fine.transpose(0, 2, 1).reshape(4 * n1, n2)
         operands = [
-            noisy, *constants[:4], bias, weights[0], w_pf, *weights[1:],
+            recv, others, noisy, *constants[:4], bias, weights[0], w_pf, *weights[1:],
             *constants[4:],
         ]
         cells = z.cells
@@ -630,7 +631,7 @@
                 jax.ShapeDtypeStruct(noisy.shape, BF),
                 jax.ShapeDtypeStruct(noisy.shape, F32),
             ),
-            in_specs=[smem, vmem, vmem] + [far] * len(operands),
+            in_specs=[smem] + [far] * len(operands),
             out_specs=(far, far),
             scratch_shapes=[pltpu.VMEM(w.shape, w.dtype) for w in operands]
             + [
@@ -638,15 +639,15 @@
                 pltpu.VMEM(noisy.shape, F32),
                 pltpu.VMEM((z.ext, cols + 128), BF),
                 pltpu.VMEM((z.gi * 40, 384), F32),
-                pltpu.VMEM((cells, 256), BF),
+                pltpu.VMEM((cells, 256), F32),
                 pltpu.VMEM((4, cells, 4 * n1), BF),
                 pltpu.VMEM((cells, 4 * n2), BF),
                 pltpu.VMEM((cells, n3), BF),
                 pltpu.VMEM((cells, z.slots * inner), BF),
-                pltpu.VMEM((cells, 3 * n3), BF),
-                pltpu.VMEM((2, cells, 4 * n2), BF),
-                pltpu.VMEM((4, cells, 6 * n1), BF),
-                pltpu.VMEM((4, cells, 6 * n1), BF),
+                pltpu.VMEM((cells, 9 * n3), BF),
+                pltpu.VMEM((4, cells, 4 * n2), BF),
+                pltpu.VMEM((6, cells, 6 * n1), BF),
+                pltpu.VMEM((6, cells, 6 * n1), BF),
                 pltpu.VMEM((rows // 4 * 24, 2 * z.step), F32),
                 pltpu.VMEM((cells, 128), F32),
                 pltpu.VMEM((cells, 128), F32),
@@ -656,7 +657,7 @@
             ],
             compiler_params=pltpu.CompilerParams(vmem_limit_bytes=63 * 2**20),
             name="net",
-        )(owner, recv, others, *operands)
+        )(owner, *operands)
 
     copied = P()
     in_specs = (

time: 41.1 us -> 39.4 us (0.959)
  Pallas kernels: 25.2 us -> 23.5 us
    pallas_call x1, Pallas kernels: 18.4 us -> 16.6 us  [shards(): pl.pallas_call(lambda *refs: net_kernel(z, len(operands), *refs), out_sha...]
where the time goes in v3:
time: 39.4 us; the launch traced here: 39.1 us
  Pallas kernels  23.5 us (60%)
  starting transfers between devices  9.15 us (23%)
  between operations  2.38 us (6%)
  waiting for transfers between devices  2.02 us (5%)
  local copies, waits for them, and re-layouts  1.4 us (4%)
  matrix products  0.65 us (2%)
    pallas_call x1, Pallas kernels, shards(): pl.pallas_call(lambda *refs: net_kernel(z, len(operands), *refs), out_sha...  16.6 us
    all_to_all x1, starting transfers between devices, shards(): recv = lax.all_to_all(send, AXES, 0, 0, tiled=True)  7.31 us
    pallas_call x1, Pallas kernels, shards(): pl.pallas_call(lambda *refs: lay_kernel(z, len(raw), *refs), out_shape=tu...  4.74 us
    pallas_call x1, Pallas kernels, shards(): pl.pallas_call(lambda *refs: pack_kernel(z, *refs), out_shape=jax.ShapeDt...  2.12 us
    all_to_all x1, waiting for transfers between devices, shards(): recv = lax.all_to_all(send, AXES, 0, 0, tiled=True)  2.02 us
    ppermute x1, starting transfers between devices, shards(): others = lax.ppermute(tile, 'plane', [(0, 1), (1, 0)])[None]  1.83 us
  transfers between devices with their start and end apart: 2, of which 1 were waited for; matrix products, arithmetic and copies ran while one was open for 3% of the time, Pallas kernels for 12%

profile of v3, /device:TPU:0, one launch (start us, length us, event | category | flops | bytes accessed | tf_op | source)
XLA Modules:
  0.0 39.1 jit_solution(17991014229693208832)
XLA Ops:
  0.6 0.0 copy-start
  0.6 2.1 %pack.1 = bf16[32,40,128]{2,1,0:T(8,128)(2,1)} custom-call(bf16[1,3,64,128]{3,2,1,0:T(8,128)(2,1)} %refs_3_.3, bf16[1,2,3,32,64]{4,3,2,1,0:T(8,128)(2,1)} %refs_1_.2), custom_call_target="tpu_custom_call" | custom-call | tf_op jit(solution)/shard_map/pack/pallas_call | solution.py:561
  2.8 7.3 %all-to-all-start = ((bf16[32,40,128]{2,1,0:T(8,128)(2,1)}), bf16[32,40,128]{2,1,0:T(8,128)(2,1)S(1)}, u32[]{:S(2)}, u32[]{:S(2)}) async-start(bf16[32,40,128]{2,1,0:T(8,128)(2,1)} %pack.1), calls=%async_computation | async-start | bytes 655360 | tf_op jit(solution)/shard_map/all_to_all | solution.py:575
  10.1 0.0 copy-start.2
  10.1 4.7 %lay.1 = (bf16[3,64,128]{2,1,0:T(8,128)(2,1)}, bf16[256,1024]{1,0:T(8,128)(2,1)}, bf16[512,256]{1,0:T(8,128)(2,1)}, bf16[256,128]{1,0:T(8,128)(2,1)}, bf16[256,2...) custom-call(bf16[1,3,64,128]{3,2,1,0:T(8,128)(2,1)} %refs_3_.3, ...), custom_call_target="tpu_custom_call" | custom-call | flops 1000000000 | bytes 10000000 | tf_op jit(solution)/shard_map/lay/pallas_call | solution.py:592
  14.9 1.8 %collective-permute-start = (bf16[3,64,128]{2,1,0:T(8,128)(2,1)}, bf16[3,64,128]{2,1,0:T(8,128)(2,1)S(1)}, u32[]{:S(2)}, u32[]{:S(2)}) collective-permute-start(bf16[3,64,128]{2,1,0:T(8,128)(2,1)} %get-tuple-element.13), channel_id=1, source_target_pairs={{0,16},{16,0},{1,17},{17,1},{2,18},{18,2},{3,19},{19,3},{4,20},{20... | collective-permute-start | bytes 147464 | tf_op jit(solution)/shard_map/ppermute | solution.py:614
  17.4 0.0 copy-done.2
  17.4 0.2 fusion
  17.6 0.0 copy-done
  17.6 0.5 %fusion.6 = f32[1,448]{1,0:T(1,128)S(1)} fusion(f32[256,1]{0,1:T(1,128)S(1)} %bitcast.23, f32[256,448]{0,1:T(8,128)S(1)} %copy-done), kind=kOutput, calls=%fused_computation.9 | convolution fusion | flops 1376256 | bytes 461568 | tf_op jit(solution)/shard_map/dot_general | solution.py:447
  19.1 0.7 %concatenate.7 = f32[452]{0:T(512)} concatenate(f32[448]{0:T(512)S(1)} %bitcast.21, f32[1]{0:T(128)} %bitcast.7, f32[1]{0:T(128)} %bitcast.8, f32[1]{0:T(128)S(6)} %sqrt.16, f32[1]{0:T(128)S(6)} %sqrt.17), dimensions={0} | concatenate | bytes 3616 | tf_op jit(solution)/shard_map/concatenate | solution.py:580
  19.8 0.0 collective-permute-done
  19.8 0.0 copy-start.3
  19.8 2.0 %all-to-all-done.refs_1_ = bf16[32,40,128]{2,1,0:T(8,128)(2,1)S(1)} async-done(((bf16[32,40,128]{2,1,0:T(8,128)(2,1)}), bf16[32,40,128]{2,1,0:T(8,128)(2,1)S(1)}, u32[]{:S(2)}, u32[]{:S(2)}) %all-to-all-start) | async-done | bytes 327712 | tf_op jit(solution)/shard_map/all_to_all | solution.py:575
  21.8 0.0 copy-start.1
  21.8 0.0 copy-done.3
  21.8 0.7 %copy-done.1 = bf16[32,40,128]{2,1,0:T(8,128)(2,1)} copy-done((bf16[32,40,128]{2,1,0:T(8,128)(2,1)}, bf16[32,40,128]{2,1,0:T(8,128)(2,1)S(1)}, u32[]{:S(2)}) %copy-start.1) | copy-done | bytes 327704
  22.5 16.6 %net.1 = (bf16[1,3,64,128]{3,2,1,0:T(8,128)(2,1)}, f32[1,3,64,128]{3,2,1,0:T(8,128)}) custom-call(s32[1]{0:T(128)S(6)} %copy.27.refs_0_, bf16[32,40,128]{2,1,0:T(8,128)(2,1)} %copy-done.1, bf16[1,3,64,128]{3,2,1,0:T(8,128)(2,1)} %bitcast.19, bf16[1,3,64,128]{3,2,1,0:T(8,128)(2,1)} %refs_3_.3, bf16[32,128]{1,0:T(8,128)(2,1)} %constant.45.clone.refs_4_, ...), custom_call_target="tpu_custom_call" | custom-call | tf_op jit(solution)/shard_map/net/pallas_call | solution.py:628
  (2 shorter events, 0.1 us)
Async XLA Ops:
  0.6 17.0 %copy-start = (f32[256,448]{0,1:T(8,128)S(1)}, f32[256,448]{0,1:T(8,128)}, u32[]{:S(2)}) copy-start(f32[256,448]{0,1:T(8,128)} %param.29) | copy-start | bytes 1376260
  2.8 19.0 %all-to-all-start = ((bf16[32,40,128]{2,1,0:T(8,128)(2,1)}), bf16[32,40,128]{2,1,0:T(8,128)(2,1)S(1)}, u32[]{:S(2)}, u32[]{:S(2)}) async-start(bf16[32,40,128]{2,1,0:T(8,128)(2,1)} %pack.1), calls=%async_computation | async-start | bytes 655360 | tf_op jit(solution)/shard_map/all_to_all | solution.py:575
  10.1 7.3 %copy-start.2 = (f32[64,256]{1,0:T(8,128)S(1)}, f32[64,256]{1,0:T(8,128)}, u32[]{:S(2)}) copy-start(f32[64,256]{1,0:T(8,128)} %param.28) | copy-start | bytes 196612
  14.9 4.9 %collective-permute-start = (bf16[3,64,128]{2,1,0:T(8,128)(2,1)}, bf16[3,64,128]{2,1,0:T(8,128)(2,1)S(1)}, u32[]{:S(2)}, u32[]{:S(2)}) collective-permute-start(bf16[3,64,128]{2,1,0:T(8,128)(2,1)} %get-tuple-element.13), channel_id=1, source_target_pairs={{0,16},{16,0},{1,17},{17,1},{2,18},{18,2},{3,19},{19,3},{4,20},{20... | collective-permute-start | bytes 147464 | tf_op jit(solution)/shard_map/ppermute | solution.py:614
  19.8 2.0 %copy-start.3 = (bf16[3,64,128]{2,1,0:T(8,128)(2,1)}, bf16[3,64,128]{2,1,0:T(8,128)(2,1)S(1)}, u32[]{:S(2)}) copy-start(bf16[3,64,128]{2,1,0:T(8,128)(2,1)S(1)} %collective-permute-done) | copy-start | bytes 147460
  21.8 0.7 %copy-start.1 = (bf16[32,40,128]{2,1,0:T(8,128)(2,1)}, bf16[32,40,128]{2,1,0:T(8,128)(2,1)S(1)}, u32[]{:S(2)}) copy-start(bf16[32,40,128]{2,1,0:T(8,128)(2,1)S(1)} %all-to-all-done.refs_1_) | copy-start | bytes 983044

commit v4 on v3

--- a/solution.py
+++ b/solution.py
@@ -334,6 +334,14 @@
     def rows_of(first, last_):
         return slice(first * step // 16 * 16, up(last_ * step, 16))
 
+    def taps(load, rows, weight, parts):
+        size = up(-(-(rows.stop - rows.start) // parts), 16)
+        out = []
+        for first in range(rows.start, rows.stop, size):
+            part = slice(first, min(first + size, rows.stop))
+            out.append(dot(jnp.concatenate(load(part), axis=1), weight[...]))
+        return out[0] if len(out) == 1 else jnp.concatenate(out, axis=0)
+
     def above(x):
         return jnp.concatenate([x[-step:], x[:-step]], axis=0)
 
@@ -354,7 +362,7 @@
 
     rows = rows_of(1, gi - 1)
     n = rows.stop - rows.start
-    c = silu(dot(mx[rows, :], w_mid[...])).astype(BF)
+    c = silu(taps(lambda part: [mx[part, :]], rows, w_mid, 2)).astype(BF)
     v = dot(c, w_rm[...]) + d1[rows, :].astype(F32)
     v = masked(v, rows)
     for p in range(2):
@@ -369,8 +377,9 @@
     for p in range(2):
         rows = rows_of(1, gi - 1 - p)
         n = rows.stop - rows.start
-        wide = [v2[at, rows, :] for at in ((2, 0, 1), (0, 1, 3))[p]]
-        e = silu(dot(jnp.concatenate(wide, axis=1), w_dm[...])).astype(BF)
+        order = ((2, 0, 1), (0, 1, 3))[p]
+        e = taps(lambda part: [v2[at, part, :] for at in order], rows, w_dm, 3)
+        e = silu(e).astype(BF)
         for q in range(2):
             v = dot(e[:, q * n2 : (q + 1) * n2], w_rf[...])
             v = masked(v + h1[2 * p + q, rows, :].astype(F32), rows)
@@ -389,8 +398,8 @@
         n = rows.stop - rows.start
         for pair in range(2):
             lanes_in = slice(2 * pair * n1, (2 * pair + 4) * n1)
-            wide = [v1[at, rows, lanes_in] for at in ((0, 1, 2, 3), (2, 3, 4, 5))[turn]]
-            x = dot(jnp.concatenate(wide, axis=1), w_df[...])
+            order = ((0, 1, 2, 3), (2, 3, 4, 5))[turn]
+            x = taps(lambda part: [v1[at, part, lanes_in] for at in order], rows, w_df, 3)
             for a in range(2):
                 shift = step if turn and a else 0
                 there = slice(rows.start + shift, rows.stop + shift)
@@ -410,8 +419,8 @@
     outs = []
     for pair in range(2):
         lanes_in = slice(2 * pair * n1, (2 * pair + 4) * n1)
-        wide = [e1[at, rows, lanes_in] for at in (4, 5, 0, 1, 2, 3)]
-        outs.append(dot(jnp.concatenate(wide, axis=1), w_lv[...]))
+        order = (4, 5, 0, 1, 2, 3)
+        outs.append(taps(lambda part: [e1[at, part, lanes_in] for at in order], rows, w_lv, 1))
     for r in range(inner):
         at = (2 + r) * step - rows.start
         block = jnp.concatenate([o[at : at + step] for o in outs], axis=0)
@@ -569,7 +578,7 @@
                 pltpu.VMEM((planes, up(z.cond_rows, 8) + 2 * z.pad, spans * 128), F32),
                 pltpu.SemaphoreType.DMA((2,)),
             ],
-            compiler_params=pltpu.CompilerParams(vmem_limit_bytes=63 * 2**20),
+            compiler_params=pltpu.CompilerParams(vmem_limit_bytes=int(63.5 * 2**20)),
             name="pack",
         )(noisy, coarse_cond)
         recv = lax.all_to_all(send, AXES, 0, 0, tiled=True)
@@ -602,7 +611,7 @@
                 pltpu.VMEM((2 * n1, 2 * n1), F32),
                 pltpu.SemaphoreType.DMA((len(raw),)),
             ],
-            compiler_params=pltpu.CompilerParams(vmem_limit_bytes=63 * 2**20),
+            compiler_params=pltpu.CompilerParams(vmem_limit_bytes=int(63.5 * 2**20)),
             cost_estimate=pl.CostEstimate(
                 flops=10**9, bytes_accessed=10**7, transcendentals=0
             ),
@@ -655,7 +664,7 @@
                 pltpu.SemaphoreType.DMA((len(operands),)),
                 pltpu.SemaphoreType.DMA((2,)),
             ],
-            compiler_params=pltpu.CompilerParams(vmem_limit_bytes=63 * 2**20),
+            compiler_params=pltpu.CompilerParams(vmem_limit_bytes=int(63.5 * 2**20)),
             name="net",
         )(owner, *operands)
 

time: 39.4 us -> 36.9 us (0.937)
  Pallas kernels: 23.5 us -> 21.5 us
  matrix products: 0.65 us -> 1.5 us
  waiting for transfers between devices: 2.02 us -> 1.24 us
  local copies, waits for them, and re-layouts: 1.4 us -> 0.68 us
    pallas_call x1, Pallas kernels: 16.6 us -> 14.7 us  [shards(): pl.pallas_call(lambda *refs: net_kernel(z, len(operands), *refs), out_sha...]
    dot_general x1, matrix products: 0.2 us -> 1.05 us  [time_bias(): jnp.dot(waves, w_embed, precision=lax.Precision.HIGHEST)]
    all_to_all x1, waiting for transfers between devices: 2.02 us -> 1.24 us  [shards(): recv = lax.all_to_all(send, AXES, 0, 0, tiled=True)]
    unnamed x8 -> x2, local copies, waits for them, and re-layouts: 0.75 us -> 0.01 us
  transfers between devices with their start and end apart: 2 -> 2, of which waited for: 1 -> 1; matrix products, arithmetic and copies ran while one was open for 3% -> 6% of each run, Pallas kernels for 12% -> 13%
where the time goes in v4:
time: 36.9 us; the launch traced here: 36.6 us
  Pallas kernels  21.5 us (58%)
  starting transfers between devices  9.19 us (25%)
  between operations  2.36 us (6%)
  matrix products  1.5 us (4%)
  waiting for transfers between devices  1.24 us (3%)
  local copies, waits for them, and re-layouts  0.68 us (2%)
    pallas_call x1, Pallas kernels, shards(): pl.pallas_call(lambda *refs: net_kernel(z, len(operands), *refs), out_sha...  14.7 us
    all_to_all x1, starting transfers between devices, shards(): recv = lax.all_to_all(send, AXES, 0, 0, tiled=True)  7.43 us
    pallas_call x1, Pallas kernels, shards(): pl.pallas_call(lambda *refs: lay_kernel(z, len(raw), *refs), out_shape=tu...  4.74 us
    pallas_call x1, Pallas kernels, shards(): pl.pallas_call(lambda *refs: pack_kernel(z, *refs), out_shape=jax.ShapeDt...  2.12 us
    ppermute x1, starting transfers between devices, shards(): others = lax.ppermute(tile, 'plane', [(0, 1), (1, 0)])[None]  1.77 us
    all_to_all x1, waiting for transfers between devices, shards(): recv = lax.all_to_all(send, AXES, 0, 0, tiled=True)  1.24 us
    dot_general x1, matrix products, time_bias(): jnp.dot(waves, w_embed, precision=lax.Precision.HIGHEST)  1.05 us
  transfers between devices with their start and end apart: 2, of which 1 were waited for; matrix products, arithmetic and copies ran while one was open for 6% of the time, Pallas kernels for 13%

profile of v4, /device:TPU:0, one launch (start us, length us, event | category | flops | bytes accessed | tf_op | source)
XLA Modules:
  0.0 36.6 jit_solution(15089118978863029337)
XLA Ops:
  0.6 0.0 copy-start
  0.6 2.1 %pack.1 = bf16[32,40,128]{2,1,0:T(8,128)(2,1)} custom-call(bf16[1,3,64,128]{3,2,1,0:T(8,128)(2,1)} %refs_3_.3, bf16[1,2,3,32,64]{4,3,2,1,0:T(8,128)(2,1)} %refs_1_.2), custom_call_target="tpu_custom_call" | custom-call | tf_op jit(solution)/shard_map/pack/pallas_call | solution.py:570
  2.8 7.4 %all-to-all-start = ((bf16[32,40,128]{2,1,0:T(8,128)(2,1)}), bf16[32,40,128]{2,1,0:T(8,128)(2,1)}, u32[]{:S(2)}, u32[]{:S(2)}) async-start(bf16[32,40,128]{2,1,0:T(8,128)(2,1)} %pack.1), calls=%async_computation | async-start | bytes 655360 | tf_op jit(solution)/shard_map/all_to_all | solution.py:584
  10.2 4.7 %lay.1 = (bf16[3,64,128]{2,1,0:T(8,128)(2,1)}, bf16[256,1024]{1,0:T(8,128)(2,1)}, bf16[512,256]{1,0:T(8,128)(2,1)}, bf16[256,128]{1,0:T(8,128)(2,1)}, bf16[256,2...) custom-call(bf16[1,3,64,128]{3,2,1,0:T(8,128)(2,1)} %refs_3_.3, ...), custom_call_target="tpu_custom_call" | custom-call | flops 1000000000 | bytes 10000000 | tf_op jit(solution)/shard_map/lay/pallas_call | solution.py:601
  15.0 1.8 %collective-permute-start = (bf16[3,64,128]{2,1,0:T(8,128)(2,1)}, bf16[3,64,128]{2,1,0:T(8,128)(2,1)}, u32[]{:S(2)}, u32[]{:S(2)}) collective-permute-start(bf16[3,64,128]{2,1,0:T(8,128)(2,1)} %get-tuple-element.13), channel_id=1, source_target_pairs={{0,16},{16,0},{1,17},{17,1},{2,18},{18,2},{3,19},{19,3},{4,20},{20... | collective-permute-start | bytes 147464 | tf_op jit(solution)/shard_map/ppermute | solution.py:623
  17.4 1.0 %fusion = f32[1,256]{1,0:T(1,128)S(1)} fusion(f32[64,256]{1,0:T(8,128)} %param.28, f32[32]{0:T(128)S(1)} %get-tuple-element.24, f32[32]{0:T(128)S(1)} %get-tuple-element.25), kind=kOutput, calls=%fused_computation.2 | convolution fusion | flops 196672 | bytes 66816 | tf_op jit(solution)/shard_map/dot_general | solution.py:455
  18.5 0.0 copy-done
  18.5 0.4 %fusion.6 = f32[1,448]{1,0:T(1,128)S(1)} fusion(f32[256,1]{0,1:T(1,128)S(1)} %bitcast.22, f32[256,448]{0,1:T(8,128)S(1)} %copy-done), kind=kOutput, calls=%fused_computation.9 | convolution fusion | flops 1376256 | bytes 461568 | tf_op jit(solution)/shard_map/dot_general | solution.py:456
  20.0 0.7 %concatenate.7 = f32[452]{0:T(512)} concatenate(f32[448]{0:T(512)S(1)} %bitcast.20, f32[1]{0:T(128)} %bitcast.7, f32[1]{0:T(128)} %bitcast.8, f32[1]{0:T(128)S(6)} %sqrt.16, f32[1]{0:T(128)S(6)} %sqrt.17), dimensions={0} | concatenate | bytes 3616 | tf_op jit(solution)/shard_map/concatenate | solution.py:589
  20.7 0.0 collective-permute-done
  20.7 1.2 %all-to-all-done.refs_1_ = bf16[32,40,128]{2,1,0:T(8,128)(2,1)} async-done(((bf16[32,40,128]{2,1,0:T(8,128)(2,1)}), bf16[32,40,128]{2,1,0:T(8,128)(2,1)}, u32[]{:S(2)}, u32[]{:S(2)}) %all-to-all-start) | async-done | bytes 327712 | tf_op jit(solution)/shard_map/all_to_all | solution.py:584
  21.9 14.7 %net.1 = (bf16[1,3,64,128]{3,2,1,0:T(8,128)(2,1)}, f32[1,3,64,128]{3,2,1,0:T(8,128)}) custom-call(s32[1]{0:T(128)S(6)} %copy.27.refs_0_, bf16[32,40,128]{2,1,0:T(8,128)(2,1)} %all-to-all-done.refs_1_, bf16[1,3,64,128]{3,2,1,0:T(8,128)(2,1)} %bitcast.1.refs_2_, bf16[1,3,64,128]{3,2,1,0:T(8,128)(2,1)} %refs_3_.3, bf16[32,128]{1,0:T(8,128)(2,1)} %constant.45.clone.refs_4_, ...), custom_call_target="tpu_custom_call" | custom-call | tf_op jit(solution)/shard_map/net/pallas_call | solution.py:637
  (2 shorter events, 0.1 us)
Async XLA Ops:
  0.6 17.9 %copy-start = (f32[256,448]{0,1:T(8,128)S(1)}, f32[256,448]{0,1:T(8,128)}, u32[]{:S(2)}) copy-start(f32[256,448]{0,1:T(8,128)} %param.29) | copy-start | bytes 1376260
  2.8 19.1 %all-to-all-start = ((bf16[32,40,128]{2,1,0:T(8,128)(2,1)}), bf16[32,40,128]{2,1,0:T(8,128)(2,1)}, u32[]{:S(2)}, u32[]{:S(2)}) async-start(bf16[32,40,128]{2,1,0:T(8,128)(2,1)} %pack.1), calls=%async_computation | async-start | bytes 655360 | tf_op jit(solution)/shard_map/all_to_all | solution.py:584
  15.0 5.7 %collective-permute-start = (bf16[3,64,128]{2,1,0:T(8,128)(2,1)}, bf16[3,64,128]{2,1,0:T(8,128)(2,1)}, u32[]{:S(2)}, u32[]{:S(2)}) collective-permute-start(bf16[3,64,128]{2,1,0:T(8,128)(2,1)} %get-tuple-element.13), channel_id=1, source_target_pairs={{0,16},{16,0},{1,17},{17,1},{2,18},{18,2},{3,19},{19,3},{4,20},{20... | collective-permute-start | bytes 147464 | tf_op jit(solution)/shard_map/ppermute | solution.py:623

commit v5 on v4

--- a/solution.py
+++ b/solution.py
@@ -254,7 +254,7 @@
         return x * jnp.concatenate([m] * (x.shape[1] // 128), axis=1)
 
     lanes = lax.broadcasted_iota(jnp.int32, (z.strip, 128), 1)
-    for copy in copies[:7]:
+    for copy in copies[:4]:
         copy.wait()
     for k in range(z.slots):
         q = z.planes_of(plane)[k]
@@ -286,6 +286,9 @@
         ext[z.strip : z.strip + 3 * z.rows, z.cols : z.cols + 128] = dot(
             rims, sides[...]
         ).astype(BF)
+        if k == 0:
+            for copy in copies[4:7]:
+                copy.wait()
         patch = recv[owner[0]].astype(F32)
         patch = jnp.concatenate([patch, jnp.zeros((z.patch - z.piece, 128), F32)], axis=0)
         patch = patch.astype(BF)
@@ -378,7 +381,7 @@
         rows = rows_of(1, gi - 1 - p)
         n = rows.stop - rows.start
         order = ((2, 0, 1), (0, 1, 3))[p]
-        e = taps(lambda part: [v2[at, part, :] for at in order], rows, w_dm, 3)
+        e = taps(lambda part: [v2[at, part, :] for at in order], rows, w_dm, 4)
         e = silu(e).astype(BF)
         for q in range(2):
             v = dot(e[:, q * n2 : (q + 1) * n2], w_rf[...])
@@ -420,7 +423,7 @@
     for pair in range(2):
         lanes_in = slice(2 * pair * n1, (2 * pair + 4) * n1)
         order = (4, 5, 0, 1, 2, 3)
-        outs.append(taps(lambda part: [e1[at, part, lanes_in] for at in order], rows, w_lv, 1))
+        outs.append(taps(lambda part: [e1[at, part, lanes_in] for at in order], rows, w_lv, 2))
     for r in range(inner):
         at = (2 + r) * step - rows.start
         block = jnp.concatenate([o[at : at + step] for o in outs], axis=0)

time: 36.9 us -> 36.7 us (level)
  no operation moved by 1% of the time
where the time goes in v5:
time: 36.7 us; the launch traced here: 36.4 us
  Pallas kernels  21.3 us (58%)
  starting transfers between devices  9.19 us (25%)
  between operations  2.36 us (6%)
  matrix products  1.5 us (4%)
  waiting for transfers between devices  1.24 us (3%)
  local copies, waits for them, and re-layouts  0.68 us (2%)
    pallas_call x1, Pallas kernels, shards(): pl.pallas_call(lambda *refs: net_kernel(z, len(operands), *refs), out_sha...  14.5 us
    all_to_all x1, starting transfers between devices, shards(): recv = lax.all_to_all(send, AXES, 0, 0, tiled=True)  7.43 us
    pallas_call x1, Pallas kernels, shards(): pl.pallas_call(lambda *refs: lay_kernel(z, len(raw), *refs), out_shape=tu...  4.74 us
    pallas_call x1, Pallas kernels, shards(): pl.pallas_call(lambda *refs: pack_kernel(z, *refs), out_shape=jax.ShapeDt...  2.12 us
    ppermute x1, starting transfers between devices, shards(): others = lax.ppermute(tile, 'plane', [(0, 1), (1, 0)])[None]  1.77 us
    all_to_all x1, waiting for transfers between devices, shards(): recv = lax.all_to_all(send, AXES, 0, 0, tiled=True)  1.24 us
    dot_general x1, matrix products, time_bias(): jnp.dot(waves, w_embed, precision=lax.Precision.HIGHEST)  1.05 us
  transfers between devices with their start and end apart: 2, of which 1 were waited for; matrix products, arithmetic and copies ran while one was open for 6% of the time, Pallas kernels for 13%

profile of v5, /device:TPU:0, one launch (start us, length us, event | category | flops | bytes accessed | tf_op | source)
XLA Modules:
  0.0 36.4 jit_solution(4343960190582483264)
XLA Ops:
  0.6 0.0 copy-start
  0.6 2.1 %pack.1 = bf16[32,40,128]{2,1,0:T(8,128)(2,1)} custom-call(bf16[1,3,64,128]{3,2,1,0:T(8,128)(2,1)} %refs_3_.3, bf16[1,2,3,32,64]{4,3,2,1,0:T(8,128)(2,1)} %refs_1_.2), custom_call_target="tpu_custom_call" | custom-call | tf_op jit(solution)/shard_map/pack/pallas_call | solution.py:573
  2.8 7.4 %all-to-all-start = ((bf16[32,40,128]{2,1,0:T(8,128)(2,1)}), bf16[32,40,128]{2,1,0:T(8,128)(2,1)}, u32[]{:S(2)}, u32[]{:S(2)}) async-start(bf16[32,40,128]{2,1,0:T(8,128)(2,1)} %pack.1), calls=%async_computation | async-start | bytes 655360 | tf_op jit(solution)/shard_map/all_to_all | solution.py:587
  10.2 4.7 %lay.1 = (bf16[3,64,128]{2,1,0:T(8,128)(2,1)}, bf16[256,1024]{1,0:T(8,128)(2,1)}, bf16[512,256]{1,0:T(8,128)(2,1)}, bf16[256,128]{1,0:T(8,128)(2,1)}, bf16[256,2...) custom-call(bf16[1,3,64,128]{3,2,1,0:T(8,128)(2,1)} %refs_3_.3, ...), custom_call_target="tpu_custom_call" | custom-call | flops 1000000000 | bytes 10000000 | tf_op jit(solution)/shard_map/lay/pallas_call | solution.py:604
  15.0 1.8 %collective-permute-start = (bf16[3,64,128]{2,1,0:T(8,128)(2,1)}, bf16[3,64,128]{2,1,0:T(8,128)(2,1)}, u32[]{:S(2)}, u32[]{:S(2)}) collective-permute-start(bf16[3,64,128]{2,1,0:T(8,128)(2,1)} %get-tuple-element.13), channel_id=1, source_target_pairs={{0,16},{16,0},{1,17},{17,1},{2,18},{18,2},{3,19},{19,3},{4,20},{20... | collective-permute-start | bytes 147464 | tf_op jit(solution)/shard_map/ppermute | solution.py:626
  17.4 1.0 %fusion = f32[1,256]{1,0:T(1,128)S(1)} fusion(f32[64,256]{1,0:T(8,128)} %param.28, f32[32]{0:T(128)S(1)} %get-tuple-element.24, f32[32]{0:T(128)S(1)} %get-tuple-element.25), kind=kOutput, calls=%fused_computation.2 | convolution fusion | flops 196672 | bytes 66816 | tf_op jit(solution)/shard_map/dot_general | solution.py:458
  18.5 0.0 copy-done
  18.5 0.4 %fusion.6 = f32[1,448]{1,0:T(1,128)S(1)} fusion(f32[256,1]{0,1:T(1,128)S(1)} %bitcast.22, f32[256,448]{0,1:T(8,128)S(1)} %copy-done), kind=kOutput, calls=%fused_computation.9 | convolution fusion | flops 1376256 | bytes 461568 | tf_op jit(solution)/shard_map/dot_general | solution.py:459
  20.0 0.7 %concatenate.7 = f32[452]{0:T(512)} concatenate(f32[448]{0:T(512)S(1)} %bitcast.20, f32[1]{0:T(128)} %bitcast.7, f32[1]{0:T(128)} %bitcast.8, f32[1]{0:T(128)S(6)} %sqrt.16, f32[1]{0:T(128)S(6)} %sqrt.17), dimensions={0} | concatenate | bytes 3616 | tf_op jit(solution)/shard_map/concatenate | solution.py:592
  20.7 0.0 collective-permute-done
  20.7 1.2 %all-to-all-done.refs_1_ = bf16[32,40,128]{2,1,0:T(8,128)(2,1)} async-done(((bf16[32,40,128]{2,1,0:T(8,128)(2,1)}), bf16[32,40,128]{2,1,0:T(8,128)(2,1)}, u32[]{:S(2)}, u32[]{:S(2)}) %all-to-all-start) | async-done | bytes 327712 | tf_op jit(solution)/shard_map/all_to_all | solution.py:587
  21.9 14.5 %net.1 = (bf16[1,3,64,128]{3,2,1,0:T(8,128)(2,1)}, f32[1,3,64,128]{3,2,1,0:T(8,128)}) custom-call(s32[1]{0:T(128)S(6)} %copy.27.refs_0_, bf16[32,40,128]{2,1,0:T(8,128)(2,1)} %all-to-all-done.refs_1_, bf16[1,3,64,128]{3,2,1,0:T(8,128)(2,1)} %bitcast.1.refs_2_, bf16[1,3,64,128]{3,2,1,0:T(8,128)(2,1)} %refs_3_.3, bf16[32,128]{1,0:T(8,128)(2,1)} %constant.45.clone.refs_4_, ...), custom_call_target="tpu_custom_call" | custom-call | tf_op jit(solution)/shard_map/net/pallas_call | solution.py:640
  (2 shorter events, 0.1 us)
Async XLA Ops:
  0.6 17.9 %copy-start = (f32[256,448]{0,1:T(8,128)S(1)}, f32[256,448]{0,1:T(8,128)}, u32[]{:S(2)}) copy-start(f32[256,448]{0,1:T(8,128)} %param.29) | copy-start | bytes 1376260
  2.8 19.1 %all-to-all-start = ((bf16[32,40,128]{2,1,0:T(8,128)(2,1)}), bf16[32,40,128]{2,1,0:T(8,128)(2,1)}, u32[]{:S(2)}, u32[]{:S(2)}) async-start(bf16[32,40,128]{2,1,0:T(8,128)(2,1)} %pack.1), calls=%async_computation | async-start | bytes 655360 | tf_op jit(solution)/shard_map/all_to_all | solution.py:587
  15.0 5.7 %collective-permute-start = (bf16[3,64,128]{2,1,0:T(8,128)(2,1)}, bf16[3,64,128]{2,1,0:T(8,128)(2,1)}, u32[]{:S(2)}, u32[]{:S(2)}) collective-permute-start(bf16[3,64,128]{2,1,0:T(8,128)(2,1)} %get-tuple-element.13), channel_id=1, source_target_pairs={{0,16},{16,0},{1,17},{17,1},{2,18},{18,2},{3,19},{19,3},{4,20},{20... | collective-permute-start | bytes 147464 | tf_op jit(solution)/shard_map/ppermute | solution.py:626
